TPU v7x, 256 devices: a whole 4x4x8 slice. The times are simulated.
256 devices in a mesh: grp: 8 (over z_lo, core), resp: 32 (over x, y, z_hi).
Axes of the slice: x: 4, y: 4, z: 8 (z_hi: 2, z_lo: 4; z = z_hi * 4 + z_lo), core: 2. Of those that a mesh axis runs over, the one named last changes fastest.
Arguments:
- hidden: bfloat16 [32768, 5120], P(('grp', 'resp')), may hold values from -6 to 6
- queries: bfloat16 [32768, 4096], P(('grp', 'resp')), may hold values from -6 to 6
- answer_token_keys: bfloat16 [32768, 512], P(('grp', 'resp')), may hold values from -6 to 6
- answer_token_values: bfloat16 [32768, 512], P(('grp', 'resp')), may hold values from -6 to 6
- cotangent: bfloat16 [32768, 4096], P(('grp', 'resp')), may hold values from -6 to 6
- slot_answer_index: int32 [32768], P(('grp', 'resp')), may hold values from -1 to 63, as said below
- rewards: float32 [8, 64], P('grp'), may hold values from -4 to 4
- group_prompt_keys: bfloat16 [16384, 512], P(('grp', 'resp')), may hold values from -6 to 6
- group_prompt_values: bfloat16 [16384, 512], P(('grp', 'resp')), may hold values from -6 to 6
- adapter_down_matrix: bfloat16 [5120, 64], replicated, may hold values from -0.078125 to 0.078125
- adapter_up_matrix: bfloat16 [64, 4096], replicated, may hold values from -0.75 to 0.75
Outputs:
- prompt_dk: bfloat16 [16384, 512], P(('grp', 'resp'))
- prompt_dv: bfloat16 [16384, 512], P(('grp', 'resp'))
- resp_dk: bfloat16 [32768, 512], P(('grp', 'resp'))
- resp_dv: bfloat16 [32768, 512], P(('grp', 'resp'))
- grad_a: float32 [5120, 64], replicated
- up_matrix_gradient: float32 [64, 4096], replicated
Inputs may be any that keep to these rules, and one draw needn't show every extreme that they name: `slot_answer_index`: the 128 slots of the device of index r along resp hold responses 2 r and 2 r + 1 of its group, in that order in consecutive slots, each 1 to 64 long, then empty slots.
All inputs are finite; a program needn't handle non-finite values.
Results may differ from a plain program's by a relative error of at most 0.013.
The roundings to bfloat16 on the way count: a program that leaves them out, or rounds other values in their place, can miss the bound.
Values may be sent and summed in bfloat16 or wider, within the bound.
A program may use at most 192 MiB of HBM per device.

v0:
```python
import jax
import jax.numpy as jnp
from jax import lax
from jax.sharding import PartitionSpec as P

HEADS = 32
KV_HEADS = 4
HEAD_DIM = 128


ADAPTER_SCALE = 2.0


def attend_back(query_h, grad_out, all_keys, all_values, visible):
    factor = query_h.shape[-1] ** (-0.5)
    scores = (
        jnp.einsum("gch,kh->gck", query_h, all_keys, preferred_element_type=jnp.float32) * factor
    )
    scores = jnp.where(visible[None], scores, -1e30)
    row_max = jnp.max(scores, axis=-1, keepdims=True)
    unnorm = jnp.exp(scores - row_max)
    probs = unnorm / jnp.sum(unnorm, axis=-1, keepdims=True)
    probs_bf = probs.astype(jnp.bfloat16)
    attended = jnp.einsum("gck,kh->gch", probs_bf, all_values, preferred_element_type=jnp.float32)
    grad_prob = jnp.einsum("gch,kh->gck", grad_out, all_values, preferred_element_type=jnp.float32)
    delta_row = jnp.sum(grad_out.astype(jnp.float32) * attended, axis=-1, keepdims=True)
    grad_score = (probs * (grad_prob - delta_row) * factor).astype(jnp.bfloat16)
    grad_query = jnp.einsum("gck,kh->gch", grad_score, all_keys, preferred_element_type=jnp.float32)
    grad_key = jnp.einsum("gck,gch->kh", grad_score, query_h, preferred_element_type=jnp.float32)
    grad_value = jnp.einsum("gck,gch->kh", probs_bf, grad_out, preferred_element_type=jnp.float32)
    return (grad_query, grad_key, grad_value)


def slot_weights(answer_slots, reward_entries_row):
    average = jnp.mean(reward_entries_row)
    spread = jnp.mean((reward_entries_row - average) * (reward_entries_row - average))
    advantage = (reward_entries_row - average) / jnp.sqrt(spread + 1e-05)
    resp_ids = jnp.arange(reward_entries_row.shape[0], dtype=jnp.int32)
    onehot = (answer_slots[:, None] == resp_ids[None, :]).astype(jnp.float32)
    counts = jnp.sum(onehot, axis=0)
    return jnp.sum(onehot * (advantage / jnp.maximum(counts, 1.0))[None, :], axis=1)


def visibility(answer_slots, prompt_len):
    row_count = answer_slots.shape[0]
    positions = jnp.arange(row_count, dtype=jnp.int32)
    same_resp = (
        (answer_slots[:, None] == answer_slots[None, :])
        & (answer_slots[:, None] >= 0)
        & (positions[None, :] <= positions[:, None])
    )
    return jnp.concatenate([jnp.ones((row_count, prompt_len), dtype=bool), same_resp], axis=1)


def body(
    hidden,
    queries,
    answer_token_keys,
    answer_token_values,
    cotangent,
    slot_answer_index,
    rewards,
    group_prompt_keys,
    group_prompt_values,
    adapter_down_matrix,
    adapter_up_matrix,
):
    prompt_key_rows, prompt_value_rows = (
        lax.all_gather(group_prompt_keys, "resp", axis=0, tiled=True),
        lax.all_gather(group_prompt_values, "resp", axis=0, tiled=True),
    )
    row_count = queries.shape[0]
    prompt_len = prompt_key_rows.shape[0]
    weights = slot_weights(slot_answer_index, rewards[0])
    grad_all = (cotangent.astype(jnp.float32) * weights[:, None]).astype(jnp.bfloat16)
    visible = visibility(slot_answer_index, prompt_len)
    group_heads = HEADS // KV_HEADS
    span = group_heads * HEAD_DIM
    query_parts, key_pre, value_pre, key_resp, value_resp = ([], [], [], [], [])
    for kv_index in range(KV_HEADS):
        query_h = (
            queries[:, kv_index * span : (kv_index + 1) * span]
            .reshape(row_count, group_heads, HEAD_DIM)
            .transpose(1, 0, 2)
        )
        grad_out = (
            grad_all[:, kv_index * span : (kv_index + 1) * span]
            .reshape(row_count, group_heads, HEAD_DIM)
            .transpose(1, 0, 2)
        )
        low_col = kv_index * HEAD_DIM
        high_col = low_col + HEAD_DIM
        all_keys = jnp.concatenate(
            [prompt_key_rows[:, low_col:high_col], answer_token_keys[:, low_col:high_col]], axis=0
        )
        all_values = jnp.concatenate(
            [prompt_value_rows[:, low_col:high_col], answer_token_values[:, low_col:high_col]],
            axis=0,
        )
        grad_query, grad_key, grad_value = attend_back(
            query_h, grad_out, all_keys, all_values, visible
        )
        query_parts.append(grad_query.transpose(1, 0, 2).reshape(row_count, span))
        key_pre.append(grad_key[:prompt_len])
        value_pre.append(grad_value[:prompt_len])
        key_resp.append(grad_key[prompt_len:])
        value_resp.append(grad_value[prompt_len:])
    owned_k, owned_v = (
        lax.psum_scatter(jnp.concatenate(key_pre, axis=1), "resp", scatter_dimension=0, tiled=True),
        lax.psum_scatter(
            jnp.concatenate(value_pre, axis=1), "resp", scatter_dimension=0, tiled=True
        ),
    )
    query_rows_gradient = jnp.concatenate(query_parts, axis=1).astype(jnp.bfloat16)
    reduced_projection = jnp.dot(
        hidden, adapter_down_matrix, preferred_element_type=jnp.float32
    ).astype(jnp.bfloat16)
    up_matrix_gradient = ADAPTER_SCALE * jnp.dot(
        reduced_projection.T, query_rows_gradient, preferred_element_type=jnp.float32
    )
    backward_reduced = (
        ADAPTER_SCALE
        * jnp.dot(query_rows_gradient, adapter_up_matrix.T, preferred_element_type=jnp.float32)
    ).astype(jnp.bfloat16)
    grad_a = jnp.dot(hidden.T, backward_reduced, preferred_element_type=jnp.float32)
    grad_a, up_matrix_gradient = lax.psum((grad_a, up_matrix_gradient), ("grp", "resp"))
    return (
        owned_k.astype(jnp.bfloat16),
        owned_v.astype(jnp.bfloat16),
        jnp.concatenate(key_resp, axis=1).astype(jnp.bfloat16),
        jnp.concatenate(value_resp, axis=1).astype(jnp.bfloat16),
        grad_a,
        up_matrix_gradient,
    )


def solution(mesh):
    in_specs = (
        P(("grp", "resp"), None),
        P(("grp", "resp"), None),
        P(("grp", "resp"), None),
        P(("grp", "resp"), None),
        P(("grp", "resp"), None),
        P(("grp", "resp")),
        P("grp", None),
        P(("grp", "resp"), None),
        P(("grp", "resp"), None),
        P(),
        P(),
    )
    out_specs = (
        P(("grp", "resp"), None),
        P(("grp", "resp"), None),
        P(("grp", "resp"), None),
        P(("grp", "resp"), None),
        P(),
        P(),
    )
    return jax.shard_map(body, mesh=mesh, in_specs=in_specs, out_specs=out_specs, check_vma=False)
```

profile of v0, /device:TPU:1, one launch (start us, length us, event | category | flops | bytes accessed | tf_op | source)
XLA Modules:
  0.0 1089.9 jit_solution(6716374335195290263)
XLA Ops:
  14.8 1.6 copy.177
  29.5 1.5 fusion.109
  32.5 73.0 %all-gather.3.cloned.1.call-done = bf16[2048,512]{1,0:T(8,128)(2,1)} async-done(((bf16[64,512]{1,0:T(8,128)(2,1)}), bf16[2048,512]{1,0:T(8,128)(2,1)}) %all-gather.3.cloned.1.call-update) | async-done | bytes 2097168 | tf_op jit(solution)/shard_map/all_gather | solution.py:69
  105.6 2.7 fusion.105
  108.3 7.5 fusion.119
  115.9 6.6 fusion.20
  122.4 72.3 %all-gather.5.cloned.1.call-done = bf16[2048,512]{1,0:T(8,128)(2,1)} async-done(((bf16[64,512]{1,0:T(8,128)(2,1)}), bf16[2048,512]{1,0:T(8,128)(2,1)}) %all-gather.5.cloned.1.call-update) | async-done | bytes 2097168 | tf_op jit(solution)/shard_map/all_gather | solution.py:70
  194.7 2.7 fusion.104
  197.4 3.7 fusion.32
  201.1 5.3 multiply_convert_fusion.3
  206.5 2.1 copy-done.4
  208.6 1.5 convolution_bitcast_fusion.8
  210.1 8.0 fusion.113
  218.2 4.4 fusion.22
  224.1 1.9 slice-done.10
  226.1 2.4 multiply_convert_fusion.1
  228.5 2.0 copy-done.5
  230.5 1.5 convolution_bitcast_fusion.6
  234.1 5.3 fusion.116
  239.5 4.4 fusion.21
  245.4 1.9 slice-done.13
  247.4 2.4 multiply_convert_fusion.2
  249.8 2.1 copy-done.6
  251.8 1.5 convolution_bitcast_fusion.7
  255.5 5.2 fusion.110
  260.7 4.4 fusion.23
  266.6 1.9 slice-done.7
  268.5 2.4 multiply_convert_fusion
  271.0 2.2 copy-done.7
  273.2 1.5 convolution_bitcast_fusion.5
  275.8 2.4 pad_maximum_fusion
  278.3 5.5 copy.296
  284.1 3.9 convolution_bitcast_fusion.4
  288.1 1.5 convolution_bitcast_fusion.2
  291.2 1.5 convolution_bitcast_fusion.3
  292.9 1.5 convolution_bitcast_fusion.1
  295.5 2.5 pad_maximum_fusion.1
  298.1 5.4 copy.298
  303.6 3.3 convolution_convert_fusion.3
  306.9 3.2 convolution_convert_fusion.1
  310.2 3.2 convolution_convert_fusion.2
  315.1 2.4 convolution_multiply_fusion
  317.5 3.2 convolution_bitcast_fusion
  327.4 193.8 %reduce-scatter.7.cloned.1.call-done = f32[64,512]{1,0:T(8,128)} async-done(((f32[2048,512]{1,0:T(8,128)}), f32[64,512]{1,0:T(8,128)}) %reduce-scatter.7.cloned.1.call-update) | async-done | bytes 131088
  523.0 257.6 %reduce-scatter.9.cloned.1.call-done = f32[64,512]{1,0:T(8,128)} async-done(((f32[2048,512]{1,0:T(8,128)}), f32[64,512]{1,0:T(8,128)}) %reduce-scatter.9.cloned.1.call-update) | async-done | bytes 131088
  782.3 296.1 %all-reduce.4.cloned.1.call-done = (f32[5120,64]{0,1:T(8,128)}, f32[64,4096]{1,0:T(8,128)}) async-done(((f32[5120,64]{0,1:T(8,128)}, f32[64,4096]{1,0:T(8,128)}), (f32[5120,64]{0,1:T(8,128)}, f32[64,4096]{1,0:T(8,128)})) %all-reduce.4.cloned.1.call-update) | async-done | bytes 2359312 | tf_op jit(solution)/shard_map/psum | solution.py:126
  1078.4 2.5 copy.306
  1080.9 2.3 copy.307
  (227 shorter events, 45.4 us)
Async XLA Ops:
  7.2 308.0 %copy-start = (bf16[128,5120]{1,0:T(8,128)(2,1)S(1)}, bf16[128,5120]{1,0:T(8,128)(2,1)}, u32[]{:S(2)}) copy-start(bf16[128,5120]{1,0:T(8,128)(2,1)} %param.11) | copy-start | bytes 3932164
  7.2 13.2 %copy-start.28 = (bf16[128,4096]{1,0:T(8,128)(2,1)S(1)}, bf16[128,4096]{1,0:T(8,128)(2,1)}, u32[]{:S(2)}) copy-start(bf16[128,4096]{1,0:T(8,128)(2,1)} %param.12) | copy-start | bytes 3145732
  7.2 98.4 %all-gather.3.cloned.1.call-start = ((), (), s32[]{:S(2)}) async-start(), calls=%async_computation.2 | async-start | bytes 2162688 | tf_op jit(solution)/shard_map/all_gather | solution.py:69
  7.9 186.8 %all-gather.5.cloned.1.call-start = ((), (), s32[]{:S(2)}) async-start(), calls=%async_computation.3 | async-start | bytes 2162688 | tf_op jit(solution)/shard_map/all_gather | solution.py:70
  8.7 512.5 %reduce-scatter.7.cloned.1.call-start = ((), (), s32[]{:S(2)}) async-start(), calls=%async_computation.4 | async-start | bytes 4325376
  16.7 8.0 copy-start.20
  16.7 14.3 %copy-start.22 = (bf16[128,1024]{0,1:T(8,128)(2,1)}, bf16[128,1024]{0,1:T(8,128)(2,1)S(1)}, u32[]{:S(2)}) copy-start(bf16[128,1024]{0,1:T(8,128)(2,1)S(1)} %get-tuple-element.43) | copy-start | bytes 786436
  16.7 14.3 %copy-start.24 = (bf16[128,1024]{0,1:T(8,128)(2,1)}, bf16[128,1024]{0,1:T(8,128)(2,1)S(1)}, u32[]{:S(2)}) copy-start(bf16[128,1024]{0,1:T(8,128)(2,1)S(1)} %get-tuple-element.42) | copy-start | bytes 786436
  16.7 14.3 %copy-start.26 = (bf16[128,1024]{0,1:T(8,128)(2,1)}, bf16[128,1024]{0,1:T(8,128)(2,1)S(1)}, u32[]{:S(2)}) copy-start(bf16[128,1024]{0,1:T(8,128)(2,1)S(1)} %get-tuple-element.40) | copy-start | bytes 786436
  16.7 12.6 %copy-start.58 = (s32[128]{0:T(128)S(1)}, s32[128]{0:T(128)}, u32[]{:S(2)}) copy-start(s32[128]{0:T(128)} %param.16) | copy-start | bytes 1540
  29.5 86.4 %copy-start.39 = (pred[128,2176]{0,1:T(8,128)(4,1)}, pred[128,2176]{0,1:T(8,128)(4,1)S(1)}, u32[]{:S(2)}) copy-start(pred[128,2176]{0,1:T(8,128)(4,1)S(1)} %concatenate.45) | copy-start | bytes 835588
  31.0 84.8 %copy-start.52 = (bf16[128,128]{1,0:T(8,128)(2,1)}, bf16[128,128]{1,0:T(8,128)(2,1)S(1)}, u32[]{:S(2)}) copy-start(bf16[128,128]{1,0:T(8,128)(2,1)S(1)} %get-tuple-element.52) | copy-start | bytes 98308
  31.0 203.1 %copy-start.49 = (bf16[128,128]{1,0:T(8,128)(2,1)}, bf16[128,128]{1,0:T(8,128)(2,1)S(1)}, u32[]{:S(2)}) copy-start(bf16[128,128]{1,0:T(8,128)(2,1)S(1)} %get-tuple-element.53) | copy-start | bytes 98308
  31.1 224.4 %copy-start.47 = (bf16[128,128]{1,0:T(8,128)(2,1)}, bf16[128,128]{1,0:T(8,128)(2,1)S(1)}, u32[]{:S(2)}) copy-start(bf16[128,128]{1,0:T(8,128)(2,1)S(1)} %get-tuple-element.54) | copy-start | bytes 98308
  108.3 7.6 copy-start.34
  115.9 81.6 %copy-start.46 = (bf16[128,8,128]{2,0,1:T(8,128)(2,1)S(1)}, bf16[128,8,128]{2,0,1:T(8,128)(2,1)}, u32[]{:S(2)}) copy-start(bf16[128,8,128]{2,0,1:T(8,128)(2,1)} %copy.178) | copy-start | bytes 786436
  115.9 81.6 %copy-start.57 = (bf16[128,128]{1,0:T(8,128)(2,1)S(1)}, bf16[128,128]{1,0:T(8,128)(2,1)}, u32[]{:S(2)}) copy-start(bf16[128,128]{1,0:T(8,128)(2,1)} %get-tuple-element.48) | copy-start | bytes 98308
  210.1 8.1 copy-start.8
  218.2 6.0 slice-start.9
  218.2 7.8 slice-start.10
  218.2 7.9 slice-start.11
  222.6 5.8 copy-start.1
  228.4 5.7 copy-start.31
  228.4 5.7 copy-start.40
  228.5 5.7 copy-start.45
  239.5 6.0 slice-start.12
  239.5 4.5 copy-start.37
  239.5 4.5 copy-start.42
  239.5 7.8 slice-start.13
  239.5 7.8 slice-start.14
  244.0 5.8 copy-start.2
  249.7 5.7 copy-start.29
  249.7 5.7 copy-start.43
  260.6 5.9 slice-start.6
  260.6 7.8 slice-start.7
  260.7 7.9 slice-start.8
  265.1 5.8 copy-start.3
  270.9 4.9 slice-start.17
  270.9 4.9 copy-start.18
  270.9 4.9 copy-start.19
  278.3 5.8 copy-start.27
  283.8 496.7 %reduce-scatter.9.cloned.1.call-start = ((), (), s32[]{:S(2)}) async-start(), calls=%async_computation.5 | async-start | bytes 4325376
  298.1 5.5 copy-start.35
  298.1 5.5 copy-start.53
  303.5 774.9 %all-reduce.4.cloned.1.call-start = ((), (), s32[]{:S(2)}) async-start(), calls=%async_computation.6 | async-start | bytes 4718592 | tf_op jit(solution)/shard_map/psum | solution.py:126
  303.6 9.9 slice-start.15
  306.9 7.5 copy-start.60
  306.9 6.6 slice-start.16
  (41 other events, 119.2 us)
Sparse Core Ops, SparseCore 0:
  11.5 94.0 all-gather.2
  109.0 85.6 all-gather.4
  283.9 237.2 reduce-scatter.6
  523.6 256.8 reduce-scatter.8
  786.5 291.9 all-reduce.3
where the time goes:
time: 1100 us; the launch traced here: 1090 us
  waiting for transfers between devices  894 us (81%)
  matrix products  77.2 us (7%)
  local copies, waits for them, and re-layouts  71.7 us (7%)
  other arithmetic  29.8 us (3%)
  between operations  16.6 us (2%)
    unnamed x7, waiting for transfers between devices  453 us
    psum x1, waiting for transfers between devices, body(): lax.psum((grad_a, up_matrix_gradient), ('grp', 'resp'))  296 us
    all_gather x1, waiting for transfers between devices, body(): lax.all_gather(group_prompt_keys, 'resp', axis=0, tiled=True)  73 us
    all_gather x1, waiting for transfers between devices, body(): lax.all_gather(group_prompt_values, 'resp', axis=0, tiled=True)  72.3 us
    unnamed x177, local copies, waits for them, and re-layouts  47.5 us
    sub x4, matrix products, attend_back(): unnorm = jnp.exp(scores - row_max)  26.1 us
  transfers between devices with their start and end apart: 5, of which 5 were waited for; matrix products, arithmetic and copies ran while one was open for 8% of the time, Pallas kernels for 0%

commit v1 on v0

v1 whole, which is shorter than its diff:
```python
import jax
import jax.numpy as jnp
from jax import lax
from jax.experimental import pallas as pl
from jax.experimental.pallas import tpu as pltpu
from jax.sharding import PartitionSpec as P

BF = jnp.bfloat16
F32 = jnp.float32
SLOTS = 128
D = 128
KVH = 4
QH = 8
SPAN = QH * D
PROMPT = 2048
RANK = 64
WIDTH = 5120
FEATURES = 4096
AW = WIDTH // KVH // 2
UW = SPAN // 2
PW = AW + UW
FACTOR = D**-0.5
LOG2E_FACTOR = FACTOR * 1.4426950408889634
NN = (((1,), (0,)), ((), ()))
NT = (((1,), (1,)), ((), ()))


def mm(a, b, dims=NN):
    return lax.dot_general(a, b, dims, preferred_element_type=F32)


def fold(x, op):
    rows, lanes = x.shape
    return op(x.reshape(rows // 8, 8, lanes), axis=0)


def lanes(start, size):
    return pl.ds(pl.multiple_of(start, 128), size)


def kernel(
    hidden, queries, ans_k, ans_v, cot, slots, rewards, prompt_k, prompt_v, down, up,
    pdk_out, pdv_out, rdk_out, rdv_out, ff_out,
    zb, kv, qb, gb, rkv, small, gfull,
    s_ref, dp_ref, ds_ref, kt, dkv, bl_send, bl, rd_send, rd, up_acc, blt,
    sb, yb, zs, zr, pf, pr, ysum,
    a_own, a_send, a_recv, u_own, u_send, u_recv, x_send, x_recv, y_send, y_recv, z_all, ff,
    send_sem, recv_sem, blk_send, blk_recv, out_send, out_recv,
):
    g = lax.axis_index("grp")
    r = lax.axis_index("resp")
    zl, core = lax.div(g, 2), lax.rem(g, 2)
    x, y, z = lax.div(r, 8), lax.rem(lax.div(r, 2), 4), lax.rem(r, 2)

    def at(gg, xx, yy, zz):
        return (gg, xx * 8 + yy * 2 + zz)

    xs = [lax.rem(x + d, 4) for d in range(4)]
    xf = [lax.rem(x + 4 - d, 4) for d in range(4)]
    ys = [lax.rem(y + d, 4) for d in range(4)]
    yf = [lax.rem(y + 4 - d, 4) for d in range(4)]
    x_dev = [at(g, xs[d], y, z) for d in range(4)]
    y_dev = [at(g, x, ys[d], z) for d in range(4)]
    z_dev = at(g, x, y, 1 - z)
    c_dev = at(zl * 2 + 1 - core, x, y, z)
    ring = []
    for dz in range(4):
        for e in range(2):
            if dz or e:
                zz = z if e == 0 else 1 - z
                ring.append((dz, e, lax.rem(zl + dz, 4), lax.rem(zl + 4 - dz, 4), zz))

    barrier = pltpu.get_barrier_semaphore()
    peers = x_dev[1:] + y_dev[1:] + [c_dev]
    peers += [at(to * 2 + core, x, y, zz) for dz, e, to, frm, zz in ring]
    for peer in peers:
        pl.semaphore_signal(barrier, inc=1, device_id=peer, device_id_type=pl.DeviceIdType.MESH)
    pl.semaphore_wait(barrier, len(peers))

    sent = []
    names = {}

    def sem(name):
        return names.setdefault(name, len(names))

    def copy(name, src, dst, dev):
        k = sem(name)
        return pltpu.make_async_remote_copy(
            src_ref=src, dst_ref=dst, send_sem=send_sem.at[k], recv_sem=recv_sem.at[k],
            device_id=dev, device_id_type=pl.DeviceIdType.MESH,
        )

    def send(name, src, dst, dev):
        c = copy(name, src, dst, dev)
        c.start()
        sent.append(c)

    def recv(name, dst, dev):
        copy(name, dst, dst, dev).wait_recv()

    def half(zz):
        return pl.ds(pl.multiple_of(zz * 64, 64), 64)

    send("z0", prompt_k, zb.at[0], z_dev)
    send("z1", prompt_v, zb.at[1], z_dev)
    for d in (1, 3, 2):
        send(("xa0", d), prompt_k.at[:, lanes(xs[d] * D, D)], kv.at[0, x, y, half(z)], x_dev[d])
        send(("xa1", d), prompt_v.at[:, lanes(xs[d] * D, D)], kv.at[1, x, y, half(z)], x_dev[d])
    kv[0, x, y, half(z), :] = prompt_k[:, lanes(x * D, D)]
    kv[1, x, y, half(z), :] = prompt_v[:, lanes(x * D, D)]

    across = jnp.broadcast_to(slots[...].astype(F32), (SLOTS, SLOTS))
    down_rows = across.T
    first = lax.broadcasted_iota(jnp.int32, (SLOTS, SLOTS), 0)
    second = lax.broadcasted_iota(jnp.int32, (SLOTS, SLOTS), 1)
    same = across == down_rows
    seen = same & (down_rows >= 0.0) & (first <= second)
    small[x, 0:SLOTS, :] = jnp.where(seen, 1.0, 0.0).astype(BF)
    reward = rewards[...]
    centred = reward - jnp.mean(reward, axis=1, keepdims=True)
    advantage = centred / jnp.sqrt(jnp.mean(centred * centred, axis=1, keepdims=True) + 1e-5)
    counts = jnp.sum(jnp.where(same, 1.0, 0.0), axis=1, keepdims=True)
    holds = down_rows[:, :64] == second[:, :64].astype(F32)
    weight = jnp.sum(jnp.where(holds, advantage, 0.0), axis=1, keepdims=True)
    weight = weight / jnp.maximum(counts, 1.0)
    for c in range(0, FEATURES, 512):
        gfull[:, c : c + 512] = (cot[:, c : c + 512].astype(F32) * weight).astype(BF)

    for d in (1, 2, 3):
        recv(("xa0", d), kv.at[0, xf[d], y, half(z)], x_dev[d])
        recv(("xa1", d), kv.at[1, xf[d], y, half(z)], x_dev[d])
    for d in (1, 2, 3):
        send(("ya", d), kv.at[:, :, y, half(z)], kv.at[:, :, y, half(z)], y_dev[d])

    low = mm(hidden[...], down[...])
    small[x, SLOTS : SLOTS + RANK, :] = low.T.astype(BF)

    recv("z0", zb.at[0], z_dev)
    recv("z1", zb.at[1], z_dev)
    for d in (1, 3, 2):
        for n in range(2):
            send(
                ("xb", n, d), zb.at[n, :, lanes(xs[d] * D, D)],
                kv.at[n, x, y, half(1 - z)], x_dev[d],
            )
    for n in range(2):
        kv[n, x, y, half(1 - z), :] = zb[n, :, lanes(x * D, D)]

    def block_copies(i, src, dev, to):
        pairs = (
            (queries.at[:, lanes(to * SPAN, SPAN)], qb.at[src]),
            (gfull.at[:, lanes(to * SPAN, SPAN)], gb.at[src]),
            (ans_k.at[:, lanes(to * D, D)], rkv.at[src, 0]),
            (ans_v.at[:, lanes(to * D, D)], rkv.at[src, 1]),
            (small.at[x], small.at[src]),
        )
        return [
            pltpu.make_async_remote_copy(
                src_ref=a, dst_ref=b, send_sem=blk_send.at[n, i], recv_sem=blk_recv.at[n, i],
                device_id=dev, device_id_type=pl.DeviceIdType.MESH,
            )
            for n, (a, b) in enumerate(pairs)
        ]

    for i, d in ((1, 1), (2, 3), (3, 2)):
        for c in block_copies(i, x, x_dev[d], xs[d]):
            c.start()
            sent.append(c)

    for d in (1, 2, 3):
        for n in range(2):
            recv(("xb", n, d), kv.at[n, xf[d], y, half(1 - z)], x_dev[d])
    for d in (1, 2, 3):
        send(("yb", d), kv.at[:, :, y, half(1 - z)], kv.at[:, :, y, half(1 - z)], y_dev[d])

    qb[x] = queries[:, lanes(x * SPAN, SPAN)]
    gb[x] = gfull[:, lanes(x * SPAN, SPAN)]
    rkv[x, 0] = ans_k[:, lanes(x * D, D)]
    rkv[x, 1] = ans_v[:, lanes(x * D, D)]
    dkv[...] = jnp.zeros_like(dkv)
    up_acc[...] = jnp.zeros_like(up_acc)
    for d in (1, 2, 3):
        recv(("ya", d), kv.at[:, :, yf[d], half(z)], y_dev[d])
    for d in (1, 2, 3):
        recv(("yb", d), kv.at[:, :, yf[d], half(1 - z)], y_dev[d])
    for c in range(16):
        kt[:, c * D : (c + 1) * D] = kv[0, c // 4, c % 4].T

    def out_copies(i, src, dev):
        pairs = ((bl_send.at[i], bl.at[src]), (rd_send.at[i], rd.at[src]))
        return [
            pltpu.make_async_remote_copy(
                src_ref=a, dst_ref=b, send_sem=out_send.at[n, i], recv_sem=out_recv.at[n, i],
                device_id=dev, device_id_type=pl.DeviceIdType.MESH,
            )
            for n, (a, b) in enumerate(pairs)
        ]

    def block(i, carry):
        step = lax.rem(lax.div(i * (i + 1), 2), 4)
        src = lax.rem(x + 4 - step, 4)

        @pl.when(i > 0)
        def _():
            for c in block_copies(i, src, at(g, src, y, z), x):
                c.wait_recv()

        kt[:, PROMPT:] = rkv[src, 0].T
        mask = small[src, 0:SLOTS, :]
        mask = jnp.concatenate([mask] * QH, axis=1) > 0
        q = jnp.concatenate([qb[src, :, j * D : (j + 1) * D] for j in range(QH)], axis=0)
        go = jnp.concatenate([gb[src, :, j * D : (j + 1) * D] for j in range(QH)], axis=0)

        def rows(n, c):
            return rkv[src, n] if c == 16 else kv[n, c // 4, c % 4]

        def span(c):
            return slice(c * D, (c + 1) * D)

        top = None
        for c in range(17):
            s = mm(rows(0, c), q, NT)
            if c == 16:
                s = jnp.where(mask, s, -1e30)
            s_ref[span(c), :] = s
            part = fold(s, jnp.max)
            top = part if top is None else jnp.maximum(top, part)
        top = jnp.max(top, axis=0, keepdims=True) * LOG2E_FACTOR
        total = None
        for c in range(17):
            e = jnp.exp2(s_ref[span(c), :] * LOG2E_FACTOR - top)
            s_ref[span(c), :] = e
            part = fold(e, jnp.sum)
            total = part if total is None else total + part
        inv = 1.0 / jnp.sum(total, axis=0, keepdims=True)
        delta = None
        for c in range(17):
            dp = mm(rows(1, c), go, NT)
            pb = (s_ref[span(c), :] * inv).astype(BF)
            dp_ref[span(c), :] = dp
            part = fold(pb.astype(F32) * dp, jnp.sum)
            delta = part if delta is None else delta + part
            gv = mm(pb, go)
            if c == 16:
                rd_send[i, 1] = gv.astype(BF)
            else:
                dkv[1, c // 4, c % 4] += gv
        delta = jnp.sum(delta, axis=0, keepdims=True)
        inv = inv * FACTOR
        for c in range(17):
            ds = (s_ref[span(c), :] * inv * (dp_ref[span(c), :] - delta)).astype(BF)
            ds_ref[span(c), :] = ds
            gk = mm(ds, q)
            if c == 16:
                rd_send[i, 0] = gk.astype(BF)
            else:
                dkv[0, c // 4, c % 4] += gk
        dq = mm(kt[...], ds_ref[...]).astype(BF)
        low_t = small[src, SLOTS : SLOTS + RANK, :]
        back = jnp.zeros((RANK, SLOTS), F32)
        for j in range(QH):
            dqj = dq[:, j * D : (j + 1) * D]
            back += mm(up[:, lanes(x * SPAN + j * D, D)], dqj)
            up_acc[:, j * D : (j + 1) * D] += mm(low_t, dqj, NT)
        bl_send[i] = back

        @pl.when(i > 0)
        def _():
            for c in out_copies(i, x, at(g, src, y, z)):
                c.start()

        return carry

    lax.fori_loop(0, 4, block, 0)
    bl[x] = bl_send[0]
    rd[x] = rd_send[0]

    sb[...] = dkv[...].astype(BF)
    for d in (1, 3, 2):
        send(("gy", d), sb.at[:, :, ys[d]], yb.at[d - 1], y_dev[d])

    for i, d in ((1, 1), (2, 3), (3, 2)):
        for c in out_copies(i, xs[d], x_dev[d]):
            c.wait_recv()
    back = 2.0 * (bl[0] + bl[1] + bl[2] + bl[3])
    blt[...] = back.astype(BF)
    mine = pl.ds(pl.multiple_of(core * 32, 32), 32)
    other = pl.ds(pl.multiple_of(32 - core * 32, 32), 32)
    bl_mine, bl_other = blt[mine, :], blt[other, :]
    for n in range(2):
        piece = up_acc[other, n * UW : (n + 1) * UW].astype(BF)
        u_send[n] = piece[0:16]
        u_send[2 + n] = piece[16:32]
    for xx in range(4):
        for n in range(2):
            cols = slice((2 * xx + n) * AW, (2 * xx + n + 1) * AW)
            piece = mm(bl_other, hidden[:, cols]).astype(BF)
            a_send[xx, n] = piece[0:16]
            a_send[xx, 2 + n] = piece[16:32]
    send("ca", a_send, a_recv, c_dev)
    send("cu", u_send, u_recv, c_dev)
    for n in range(2):
        piece = up_acc[mine, n * UW : (n + 1) * UW]
        u_own[n] = piece[0:16]
        u_own[2 + n] = piece[16:32]
    for xx in range(4):
        for n in range(2):
            cols = slice((2 * xx + n) * AW, (2 * xx + n + 1) * AW)
            piece = mm(bl_mine, hidden[:, cols])
            a_own[xx, n] = piece[0:16]
            a_own[xx, 2 + n] = piece[16:32]
    recv("ca", a_recv, c_dev)
    for xx in range(4):
        part = a_own[xx] + a_recv[xx].astype(F32)
        a_own[xx] = part
        x_send[xx] = part.astype(BF)
    for d in (1, 3, 2):
        send(("rx", d), x_send.at[xs[d]], x_recv.at[d - 1], x_dev[d])
    recv("cu", u_recv, c_dev)
    u_sum = u_own[...] + u_recv[...].astype(F32)

    for d in (1, 2, 3):
        recv(("gy", d), yb.at[d - 1], y_dev[d])
    for n in range(2):
        for xx in range(4):
            part = dkv[n, xx, y]
            for d in range(3):
                part += yb[d, n, xx].astype(F32)
            ysum[n, xx] = part
            sb[n, xx, y] = part.astype(BF)
    send("gz", sb.at[:, :, y, half(1 - z)], zr, z_dev)

    for d in (1, 2, 3):
        recv(("rx", d), x_recv.at[d - 1], x_dev[d])
    a_sum = a_own[x]
    for d in range(3):
        a_sum += x_recv[d].astype(F32)
    y_send[:, :, 0:AW] = a_sum.astype(BF)
    y_send[:, :, AW:PW] = (2.0 * u_sum).astype(BF)
    ysum_a = a_sum
    a_own[x] = ysum_a
    u_own[...] = 2.0 * u_sum
    for d in (1, 3, 2):
        send(("ry", d), y_send.at[ys[d]], y_recv.at[d - 1], y_dev[d])
    for d in (1, 2, 3):
        recv(("ry", d), y_recv.at[d - 1], y_dev[d])
    part_a = a_own[x, y]
    part_u = u_own[y]
    for d in range(3):
        part_a += y_recv[d, :, 0:AW].astype(F32)
        part_u += y_recv[d, :, AW:PW].astype(F32)
    here = zl * 2 + z
    z_all[here, :, 0:AW] = part_a.astype(BF)
    z_all[here, :, AW:PW] = part_u.astype(BF)
    for dz, e, to, frm, zz in ring:
        send(("rz", dz, e), z_all.at[here], z_all.at[here], at(to * 2 + core, x, y, zz))

    recv("gz", zr, z_dev)
    for n in range(2):
        for xx in range(4):
            part = ysum[n, xx, half(z), :] + zr[n, xx].astype(F32)
            pf[xx, n] = part.astype(BF)
    for d in (1, 3, 2):
        send(("gx", d), pf.at[xs[d]], pr.at[x], x_dev[d])
    pr[x] = pf[x]

    for dz, e, to, frm, zz in ring:
        recv(("rz", dz, e), z_all.at[frm * 2 + zz], at(to * 2 + core, x, y, zz))
    total = z_all[0].astype(F32)
    for n in range(1, 8):
        total += z_all[n].astype(F32)
    ff[core, x, y] = total.astype(BF)
    for d in (1, 3, 2):
        send(("fy", d), ff.at[core, x, y], ff.at[core, x, y], y_dev[d])
    for h in range(4):
        rdk_out[:, h * D : (h + 1) * D] = rd[h, 0]
        rdv_out[:, h * D : (h + 1) * D] = rd[h, 1]
    for d in (1, 2, 3):
        recv(("gx", d), pr.at[xf[d]], x_dev[d])
    for h in range(4):
        pdk_out[:, h * D : (h + 1) * D] = pr[h, 0]
        pdv_out[:, h * D : (h + 1) * D] = pr[h, 1]
    for d in (1, 2, 3):
        recv(("fy", d), ff.at[core, x, yf[d]], y_dev[d])
    for d in (1, 3, 2):
        send(("fx", d), ff.at[core, x], ff.at[core, x], x_dev[d])
    send(("fc", 0), ff.at[core, x], ff.at[core, x], c_dev)
    for d in (1, 3, 2):
        recv(("fx", d), ff.at[core, xf[d]], x_dev[d])
        send(("fc", d), ff.at[core, xf[d]], ff.at[core, xf[d]], c_dev)
    for d in range(4):
        recv(("fc", d), ff.at[1 - core, xf[d]], c_dev)
    ff_out[...] = ff[...]

    for c in sent:
        c.wait_send()
    for i, d in ((1, 1), (2, 3), (3, 2)):
        for c in out_copies(i, x, x_dev[0]):
            c.wait_send()


def body(
    hidden, queries, answer_token_keys, answer_token_values, cotangent, slot_answer_index,
    rewards, group_prompt_keys, group_prompt_values, adapter_down_matrix, adapter_up_matrix,
):
    vmem = pl.BlockSpec(memory_space=pltpu.VMEM)
    v = pltpu.VMEM
    scratch = [
        v((2, 64, 512), BF), v((2, 4, 4, 128, D), BF),
        v((4, SLOTS, SPAN), BF), v((4, SLOTS, SPAN), BF), v((4, 2, SLOTS, D), BF),
        v((4, SLOTS + RANK, 128), BF), v((SLOTS, FEATURES), BF),
        v((PROMPT + SLOTS, SPAN), F32), v((PROMPT + SLOTS, SPAN), F32),
        v((PROMPT + SLOTS, SPAN), BF), v((D, PROMPT + SLOTS), BF),
        v((2, 4, 4, 128, D), F32),
        v((4, RANK, SLOTS), F32), v((4, RANK, SLOTS), F32),
        v((4, 2, SLOTS, D), BF), v((4, 2, SLOTS, D), BF),
        v((RANK, SPAN), F32), v((RANK, SLOTS), BF),
        v((2, 4, 4, 128, D), BF), v((3, 2, 4, 128, D), BF), v((16, 128), BF),
        v((2, 4, 64, D), BF), v((4, 2, 64, D), BF), v((4, 2, 64, D), BF),
        v((2, 4, 128, D), F32),
        v((4, 4, 16, AW), F32), v((4, 4, 16, AW), BF), v((4, 4, 16, AW), BF),
        v((4, 16, UW), F32), v((4, 16, UW), BF), v((4, 16, UW), BF),
        v((4, 4, 16, AW), BF), v((3, 4, 16, AW), BF),
        v((4, 16, PW), BF), v((3, 16, PW), BF), v((8, 16, PW), BF),
        v((2, 4, 4, 16, PW), BF),
        pltpu.SemaphoreType.DMA((64,)), pltpu.SemaphoreType.DMA((64,)),
        pltpu.SemaphoreType.DMA((5, 4)), pltpu.SemaphoreType.DMA((5, 4)),
        pltpu.SemaphoreType.DMA((2, 4)), pltpu.SemaphoreType.DMA((2, 4)),
    ]
    pdk, pdv, rdk, rdv, ff = pl.pallas_call(
        kernel,
        out_shape=[
            jax.ShapeDtypeStruct((64, 512), BF), jax.ShapeDtypeStruct((64, 512), BF),
            jax.ShapeDtypeStruct((128, 512), BF), jax.ShapeDtypeStruct((128, 512), BF),
            jax.ShapeDtypeStruct((2, 4, 4, 16, PW), BF),
        ],
        in_specs=[vmem] * 11,
        out_specs=[vmem] * 5,
        scratch_shapes=scratch,
        compiler_params=pltpu.CompilerParams(
            collective_id=0, has_side_effects=True, vmem_limit_bytes=60 << 20
        ),
    )(
        hidden, queries, answer_token_keys, answer_token_values, cotangent,
        slot_answer_index.reshape(1, SLOTS), rewards, group_prompt_keys, group_prompt_values,
        adapter_down_matrix, adapter_up_matrix,
    )
    pieces = ff.reshape(2, 4, 2, 2, 16, PW)
    grad_a = pieces[..., :AW].transpose(1, 3, 5, 0, 2, 4).reshape(WIDTH, RANK).astype(F32)
    grad_up = pieces[..., AW:].transpose(0, 2, 4, 1, 3, 5).reshape(RANK, FEATURES).astype(F32)
    return pdk, pdv, rdk, rdv, grad_a, grad_up


def solution(mesh):
    rows = P(("grp", "resp"), None)
    in_specs = (
        rows, rows, rows, rows, rows, P(("grp", "resp")), P("grp", None), rows, rows, P(), P(),
    )
    out_specs = (rows, rows, rows, rows, P(), P())
    return jax.shard_map(body, mesh=mesh, in_specs=in_specs, out_specs=out_specs, check_vma=False)
```

time: 1100 us -> 126 us (0.11)
  waiting for transfers between devices: 894 us -> 0 us
  Pallas kernels: 0 us -> 113 us
  matrix products: 77.2 us -> 0 us
  local copies, waits for them, and re-layouts: 71.7 us -> 10.4 us
  other arithmetic: 29.8 us -> 1.29 us
  between operations: 16.6 us -> 0.72 us
    unnamed x7 -> x0, waiting for transfers between devices: 453 us -> none
    psum x1 -> x0, waiting for transfers between devices: 296 us -> none  [body(): lax.psum((grad_a, up_matrix_gradient), ('grp', 'resp'))]
    all_gather x2 -> x0, waiting for transfers between devices: 145 us -> none  [the longest x1 73 us: body(): lax.all_gather(group_prompt_keys, 'resp', axis=0, tiled=True)]
    pallas_call x0 -> x1, Pallas kernels: none -> 113 us  [body(): pl.pallas_call(kernel, out_shape=[jax.ShapeDtypeStruct((64, 512), BF), ja...]
    dot_general x22 -> x0, matrix products: 51.1 us -> none  [the longest x4 12.4 us: attend_back(): jnp.einsum('gch,kh->gck', grad_out, all_values, preferred_element_type=jn...]
    unnamed x177 -> x15, local copies, waits for them, and re-layouts: 47.5 us -> 4.91 us
    sub x4 -> x0, matrix products: 26.1 us -> none  [attend_back(): unnorm = jnp.exp(scores - row_max)]
    convert_element_type x5 -> x2, other arithmetic: 20 us -> 1.29 us  [the longest x1 1.16 us: body(): pieces[..., AW:].transpose(0, 2, 4, 1, 3, 5).reshape(RANK, FEATURES)]
  transfers between devices with their start and end apart: 5 -> 0, of which waited for: 5 -> 0; matrix products, arithmetic and copies ran while one was open for 8% -> 0% of each run, Pallas kernels for 0% -> 0%
where the time goes in v1:
time: 126 us
  Pallas kernels  113 us (90%)
  local copies, waits for them, and re-layouts  10.4 us (8%)
  other arithmetic  1.29 us (1%)
    pallas_call x1, Pallas kernels, body(): pl.pallas_call(kernel, out_shape=[jax.ShapeDtypeStruct((64, 512), BF), ja...  113 us
    unnamed x15, local copies, waits for them, and re-layouts  4.91 us
    convert_element_type x2, local copies, waits for them, and re-layouts, body(): pieces[..., :AW].transpose(1, 3, 5, 0, 2, 4).reshape(WIDTH, RANK)  2.78 us
    convert_element_type x2, local copies, waits for them, and re-layouts, body(): pieces[..., AW:].transpose(0, 2, 4, 1, 3, 5).reshape(RANK, FEATURES)  2.68 us

profile of v1, /device:TPU:1, one launch (start us, length us, event | category | flops | bytes accessed | tf_op | source)
XLA Modules:
  0.0 125.5 jit_solution(15654369921972609335)
XLA Ops:
  0.6 2.3 %copy.17.down = bf16[5120,64]{1,0:T(8,128)(2,1)} copy(bf16[5120,64]{0,1:T(8,128)(2,1)} %param.20) | data formatting | bytes 1310720 | tf_op args[9]
  2.9 113.2 %shard_map.154 = (bf16[64,512]{1,0:T(8,128)(2,1)}, bf16[64,512]{1,0:T(8,128)(2,1)}, bf16[128,512]{1,0:T(8,128)(2,1)}, bf16[128,512]{1,0:T(8,128)(2,1)}, bf16[2,4,4,16,1152]{4,3,2,1,0:T(8,128)(2,1)}) custom-call(bf16[128,5120]{1,0:T(8,128)(2,1)} %hidden.1, bf16[128,4096]{1,0:T(8,128)(2,1)} %queries.1, bf16[128,512]{1,0:T(8,128)(2,1)} %ans_k.1, ...), custom_call_target="tpu_custom_call" | custom-call | tf_op jit(solution)/shard_map/pallas_call | solution.py:430
  116.1 1.2 convert_bitcast_fusion.1
  117.3 0.8 copy.19
  118.1 0.0 copy-start
  118.1 1.9 %reshape.27 = f32[64,4096]{1,0:T(8,128)} reshape(f32[2,2,16,4,2,512]{5,4,3,2,1,0:T(2,128)S(1)} %copy.19) | data formatting | bytes 2097152 | tf_op jit(solution)/shard_map/convert_element_type | solution.py:450
  120.0 0.0 copy-done
  120.0 0.1 convert_bitcast_fusion
  120.1 0.7 copy.18
  120.8 0.0 copy-start.4
  120.8 0.0 copy-start.3
  120.8 0.0 copy-start.2
  120.8 0.0 copy-start.1
  120.8 2.1 %reshape.26 = f32[5120,64]{0,1:T(8,128)} reshape(f32[4,2,640,2,2,16]{2,1,0,5,4,3:T(2,128)S(1)} %copy.18) | data formatting | bytes 2621440 | tf_op jit(solution)/shard_map/convert_element_type | solution.py:449
  122.9 0.0 copy-done.4
  122.9 0.6 copy.24
  123.6 0.0 copy-done.3
  123.6 0.6 copy.25
  124.2 0.0 copy-done.2
  124.2 0.7 copy.26
  124.9 0.0 copy-done.1
  124.9 0.7 copy.27
Async XLA Ops:
  118.1 1.9 %copy-start = (bf16[2,4,4,16,1152]{4,3,2,1,0:T(8,128)(2,1)S(1)}, bf16[2,4,4,16,1152]{4,3,2,1,0:T(8,128)(2,1)}, u32[]{:S(2)}) copy-start(bf16[2,4,4,16,1152]{4,3,2,1,0:T(8,128)(2,1)} %get-tuple-element.15) | copy-start | bytes 3538948
  120.8 2.1 %copy-start.4 = (bf16[64,512]{1,0:T(8,128)(2,1)S(1)}, bf16[64,512]{1,0:T(8,128)(2,1)}, u32[]{:S(2)}) copy-start(bf16[64,512]{1,0:T(8,128)(2,1)} %get-tuple-element.22) | copy-start | bytes 196612
  120.8 2.8 %copy-start.3 = (bf16[64,512]{1,0:T(8,128)(2,1)S(1)}, bf16[64,512]{1,0:T(8,128)(2,1)}, u32[]{:S(2)}) copy-start(bf16[64,512]{1,0:T(8,128)(2,1)} %get-tuple-element.23) | copy-start | bytes 196612
  120.8 3.4 %copy-start.2 = (bf16[128,512]{1,0:T(8,128)(2,1)S(1)}, bf16[128,512]{1,0:T(8,128)(2,1)}, u32[]{:S(2)}) copy-start(bf16[128,512]{1,0:T(8,128)(2,1)} %get-tuple-element.24) | copy-start | bytes 393220
  120.8 4.0 %copy-start.1 = (bf16[128,512]{1,0:T(8,128)(2,1)S(1)}, bf16[128,512]{1,0:T(8,128)(2,1)}, u32[]{:S(2)}) copy-start(bf16[128,512]{1,0:T(8,128)(2,1)} %get-tuple-element.25) | copy-start | bytes 393220

commit v2 on v1

v2 whole, which is shorter than its diff:
```python
import jax
import jax.numpy as jnp
from jax import lax
from jax.experimental import pallas as pl
from jax.experimental.pallas import tpu as pltpu
from jax.sharding import PartitionSpec as P

BF = jnp.bfloat16
F32 = jnp.float32
SLOTS = 128
D = 128
KVH = 4
QH = 8
SPAN = QH * D
PROMPT = 2048
RANK = 64
WIDTH = 5120
FEATURES = 4096
AW = WIDTH // KVH // 2
UW = SPAN // 2
PW = AW + UW
HW = WIDTH // KVH
FACTOR = D**-0.5
LOG2E_FACTOR = FACTOR * 1.4426950408889634
NN = (((1,), (0,)), ((), ()))
NT = (((1,), (1,)), ((), ()))


def mm(a, b, dims=NN):
    return lax.dot_general(a, b, dims, preferred_element_type=F32)


def fold(x, op):
    rows, lanes = x.shape
    return op(x.reshape(rows // 8, 8, lanes), axis=0)


def lanes(start, size):
    return pl.ds(pl.multiple_of(start, 128), size)


def kernel(
    hidden, queries, ans_k, ans_v, cot, slots, rewards, prompt_k, prompt_v, down_t, up,
    grads_out, ff_out,
    hid, down_v, up_v, cot_v, pk, pv, zb, kv, qb, gb, hb, rkv, masks, lows, gfull,
    s_ref, dp_ref, ds_ref, kt, dkv, bl, rd_send, rd, up_acc, blt,
    sb, yb, zr, pf, pr, ysum,
    g_own, g_send, g_recv, z_all, ff,
    send_sem, recv_sem, blk_send, blk_recv, bl_send, bl_recv, rd_send_sem, rd_recv_sem, local_sem,
):
    g = lax.axis_index("grp")
    r = lax.axis_index("resp")
    zl, core = lax.div(g, 2), lax.rem(g, 2)
    x, y, z = lax.div(r, 8), lax.rem(lax.div(r, 2), 4), lax.rem(r, 2)
    mesh_id = pl.DeviceIdType.MESH

    def at(gg, xx, yy, zz):
        return (gg, xx * 8 + yy * 2 + zz)

    xs = [lax.rem(x + d, 4) for d in range(4)]
    xf = [lax.rem(x + 4 - d, 4) for d in range(4)]
    ys = [lax.rem(y + d, 4) for d in range(4)]
    yf = [lax.rem(y + 4 - d, 4) for d in range(4)]
    x_dev = [at(g, xs[d], y, z) for d in range(4)]
    y_dev = [at(g, x, ys[d], z) for d in range(4)]
    z_dev = at(g, x, y, 1 - z)
    other_g = zl * 2 + 1 - core
    c_dev = at(other_g, x, y, z)
    ring = []
    for dz in range(4):
        for e in range(2):
            if dz or e:
                zz = z if e == 0 else 1 - z
                ring.append((dz, e, lax.rem(zl + dz, 4), lax.rem(zl + 4 - dz, 4), zz))
    column = []
    for dc in range(2):
        for dy in range(4):
            if dc or dy:
                column.append((dc, dy, core if dc == 0 else 1 - core, g if dc == 0 else other_g))
    plane = []
    for dx in (0, 1, 3, 2):
        for dy in (0, 1, 3, 2):
            if dx or dy:
                plane.append((dx, dy))

    def fetch(n, src, dst):
        c = pltpu.make_async_copy(src, dst, local_sem.at[n])
        c.start()
        return c

    loads = [
        fetch(0, prompt_k.at[:, lanes(x * D, D)], pk),
        fetch(1, prompt_v.at[:, lanes(x * D, D)], pv),
        fetch(2, cot, cot_v),
        fetch(3, hidden, hid),
        fetch(4, down_t, down_v),
        fetch(5, queries.at[:, lanes(x * SPAN, SPAN)], qb.at[x]),
        fetch(6, ans_k.at[:, lanes(x * D, D)], rkv.at[x, 0]),
        fetch(7, ans_v.at[:, lanes(x * D, D)], rkv.at[x, 1]),
        fetch(8, up.at[:, lanes(x * SPAN, SPAN)], up_v),
        fetch(9, hidden.at[:, lanes(x * HW, HW)], hb.at[x]),
    ]

    barrier = pltpu.get_barrier_semaphore()
    peers = [at(to * 2 + core, x, y, zz) for dz, e, to, frm, zz in ring]
    peers += [at(gg, x, ys[dy], z) for dc, dy, cc, gg in column]
    peers += [at(g, xs[dx], ys[dy], z) for dx, dy in plane if dx]
    for peer in peers:
        pl.semaphore_signal(barrier, inc=1, device_id=peer, device_id_type=mesh_id)
    pl.semaphore_wait(barrier, len(peers))

    sent = []
    names = {}

    def copy(name, src, dst, dev):
        k = names.setdefault(name, len(names))
        return pltpu.make_async_remote_copy(
            src_ref=src, dst_ref=dst, send_sem=send_sem.at[k], recv_sem=recv_sem.at[k],
            device_id=dev, device_id_type=mesh_id,
        )

    def send(name, src, dst, dev):
        c = copy(name, src, dst, dev)
        c.start()
        sent.append(c)

    def recv(name, dst, dev):
        copy(name, dst, dst, dev).wait_recv()

    def half(zz):
        return pl.ds(pl.multiple_of(zz * 64, 64), 64)

    def x_send(part, n, source, zz):
        for d in (1, 3, 2):
            send(
                ("x", part, n, d), source.at[:, lanes(xs[d] * D, D)],
                kv.at[n, x, y, half(zz)], x_dev[d],
            )

    def x_recv(part, n, zz):
        for d in (1, 2, 3):
            recv(("x", part, n, d), kv.at[n, xf[d], y, half(zz)], x_dev[d])

    def y_send(part, n, zz):
        for d in (1, 2, 3):
            send(("y", part, n, d), kv.at[n, :, y, half(zz)], kv.at[n, :, y, half(zz)], y_dev[d])

    def y_recv(part, n, zz):
        for d in (1, 2, 3):
            recv(("y", part, n, d), kv.at[n, :, yf[d], half(zz)], y_dev[d])

    send(("z", 0), prompt_k, zb.at[0], z_dev)
    x_send(0, 0, prompt_k, z)
    send(("z", 1), prompt_v, zb.at[1], z_dev)
    x_send(0, 1, prompt_v, z)

    across = jnp.broadcast_to(slots[...].astype(F32), (SLOTS, SLOTS))
    down_rows = across.T
    first = lax.broadcasted_iota(jnp.int32, (SLOTS, SLOTS), 0)
    second = lax.broadcasted_iota(jnp.int32, (SLOTS, SLOTS), 1)
    same = across == down_rows
    seen = same & (down_rows >= 0.0) & (first <= second)
    masks[x] = jnp.where(seen, 1.0, 0.0).astype(BF)
    reward = rewards[...]
    centred = reward - jnp.mean(reward, axis=1, keepdims=True)
    advantage = centred / jnp.sqrt(jnp.mean(centred * centred, axis=1, keepdims=True) + 1e-5)
    counts = jnp.sum(jnp.where(same, 1.0, 0.0), axis=1, keepdims=True)
    holds = down_rows[:, :64] == second[:, :64].astype(F32)
    weight = jnp.sum(jnp.where(holds, advantage, 0.0), axis=1, keepdims=True)
    weight = weight / jnp.maximum(counts, 1.0)
    loads[0].wait()
    loads[1].wait()
    kv[0, x, y, half(z), :] = pk[...]
    kv[1, x, y, half(z), :] = pv[...]
    x_recv(0, 0, z)
    y_send(0, 0, z)
    loads[2].wait()
    for c in range(0, FEATURES, 512):
        gfull[:, c : c + 512] = (cot_v[:, c : c + 512].astype(F32) * weight).astype(BF)
    x_recv(0, 1, z)
    y_send(0, 1, z)
    recv(("z", 0), zb.at[0], z_dev)
    x_send(1, 0, zb.at[0], 1 - z)
    kv[0, x, y, half(1 - z), :] = zb[0, :, lanes(x * D, D)]
    x_recv(1, 0, 1 - z)
    y_send(1, 0, 1 - z)
    recv(("z", 1), zb.at[1], z_dev)
    x_send(1, 1, zb.at[1], 1 - z)
    kv[1, x, y, half(1 - z), :] = zb[1, :, lanes(x * D, D)]

    def block_copies(i, src, dev, to):
        pairs = (
            (queries.at[:, lanes(to * SPAN, SPAN)], qb.at[src]),
            (gfull.at[:, lanes(to * SPAN, SPAN)], gb.at[src]),
            (ans_k.at[:, lanes(to * D, D)], rkv.at[src, 0]),
            (ans_v.at[:, lanes(to * D, D)], rkv.at[src, 1]),
            (masks.at[x], masks.at[src]),
            (lows.at[x], lows.at[src]),
            (hidden.at[:, lanes(to * HW, HW)], hb.at[src]),
        )
        return [
            pltpu.make_async_remote_copy(
                src_ref=a, dst_ref=b, send_sem=blk_send.at[n, i], recv_sem=blk_recv.at[n, i],
                device_id=dev, device_id_type=mesh_id,
            )
            for n, (a, b) in enumerate(pairs)
        ]

    x_recv(1, 1, 1 - z)
    y_send(1, 1, 1 - z)
    steps = ((1, 1), (2, 3), (3, 2))
    def block_send(i, d, which):
        for c in block_copies(i, x, x_dev[d], xs[d])[which]:
            c.start()

    block_send(1, 1, slice(0, 5))
    block_send(2, 3, slice(0, 5))
    loads[3].wait()
    loads[4].wait()
    lows[x] = mm(down_v[...], hid[...], NT).astype(BF)
    for i, d in steps:
        block_send(i, d, slice(5, 6))

    gb[x] = gfull[:, lanes(x * SPAN, SPAN)]
    dkv[...] = jnp.zeros_like(dkv)
    up_acc[...] = jnp.zeros_like(up_acc)
    for n in range(5, 10):
        loads[n].wait()
    y_recv(0, 0, z)
    y_recv(1, 0, 1 - z)

    def rd_copy(i, src, dev):
        return pltpu.make_async_remote_copy(
            src_ref=rd_send.at[i], dst_ref=rd.at[src],
            send_sem=rd_send_sem.at[i], recv_sem=rd_recv_sem.at[i],
            device_id=dev, device_id_type=mesh_id,
        )

    def bl_copy(i, d, head, block):
        return pltpu.make_async_remote_copy(
            src_ref=bl.at[head, block], dst_ref=bl.at[head, block],
            send_sem=bl_send.at[d, i], recv_sem=bl_recv.at[d, i],
            device_id=x_dev[d], device_id_type=mesh_id,
        )

    def step_of(i):
        return lax.rem(lax.div(i * (i + 1), 2), 4)

    def block(i, carry):
        src = lax.rem(x + 4 - step_of(i), 4)

        @pl.when(i > 0)
        def _():
            for c in block_copies(i, src, at(g, src, y, z), x)[:5]:
                c.wait_recv()

        @pl.when(i == 1)
        def _():
            block_send(3, 2, slice(0, 5))

        @pl.when(i == 2)
        def _():
            for n, d in steps:
                block_send(n, d, slice(6, 7))

        kt[:, PROMPT:] = rkv[src, 0].T
        mask = masks[src]
        mask = jnp.concatenate([mask] * QH, axis=1) > 0
        q = jnp.concatenate([qb[src, :, j * D : (j + 1) * D] for j in range(QH)], axis=0)
        go = jnp.concatenate([gb[src, :, j * D : (j + 1) * D] for j in range(QH)], axis=0)

        def rows(n, c):
            return rkv[src, n] if c == 16 else kv[n, c // 4, c % 4]

        def span(c):
            return slice(c * D, (c + 1) * D)

        top = None
        for c in range(17):
            s = mm(rows(0, c), q, NT)
            if c == 16:
                s = jnp.where(mask, s, -1e30)
            s_ref[span(c), :] = s
            part = fold(s, jnp.max)
            top = part if top is None else jnp.maximum(top, part)
        top = jnp.max(top, axis=0, keepdims=True) * LOG2E_FACTOR
        total = None
        for c in range(17):
            e = jnp.exp2(s_ref[span(c), :] * LOG2E_FACTOR - top)
            s_ref[span(c), :] = e
            part = fold(e, jnp.sum)
            total = part if total is None else total + part
        inv = 1.0 / jnp.sum(total, axis=0, keepdims=True)

        @pl.when(i == 0)
        def _():
            for c in range(16):
                kt[:, c * D : (c + 1) * D] = kv[0, c // 4, c % 4].T
            y_recv(0, 1, z)
            y_recv(1, 1, 1 - z)

        delta = None
        for c in range(17):
            dp = mm(rows(1, c), go, NT)
            pb = (s_ref[span(c), :] * inv).astype(BF)
            dp_ref[span(c), :] = dp
            part = fold(pb.astype(F32) * dp, jnp.sum)
            delta = part if delta is None else delta + part
            gv = mm(pb, go)
            if c == 16:
                rd_send[i, 1] = gv.astype(BF)
            else:
                dkv[1, c // 4, c % 4] += gv
        delta = jnp.sum(delta, axis=0, keepdims=True)
        inv = inv * FACTOR

        @pl.when(i == 3)
        def _():
            sb[1] = dkv[1].astype(BF)
            for d in (1, 3, 2):
                copy(("gy", 1, d), sb.at[1, :, ys[d]], yb.at[1, d - 1], y_dev[d]).start()

        for c in range(17):
            ds = (s_ref[span(c), :] * inv * (dp_ref[span(c), :] - delta)).astype(BF)
            ds_ref[span(c), :] = ds
        dq = mm(kt[...], ds_ref[...]).astype(BF)
        back = jnp.zeros((RANK, SLOTS), F32)
        for j in range(QH):
            back += mm(up_v[:, j * D : (j + 1) * D], dq[:, j * D : (j + 1) * D])
        bl[x, src] = back
        for d in (1, 3, 2):
            bl_copy(i, d, x, src).start()

        @pl.when(i > 0)
        def _():
            block_copies(i, src, at(g, src, y, z), x)[5].wait_recv()

        for c in range(17):
            gk = mm(ds_ref[span(c), :], q)
            if c == 16:
                rd_send[i, 0] = gk.astype(BF)
            else:
                dkv[0, c // 4, c % 4] += gk
        low_t = lows[src]
        for j in range(QH):
            up_acc[:, j * D : (j + 1) * D] += mm(low_t, dq[:, j * D : (j + 1) * D], NT)

        @pl.when(i > 0)
        def _():
            rd_copy(i, x, at(g, src, y, z)).start()

        return carry

    lax.fori_loop(0, 4, block, 0)
    for d in (1, 3, 2):
        sent.append(copy(("gy", 1, d), sb.at[1, :, ys[d]], yb.at[1, d - 1], y_dev[d]))

    rd[x] = rd_send[0]
    sb[0] = dkv[0].astype(BF)
    for n in range(2):
        for h in range(2):
            for c in range(2):
                rows = slice(c * 32 + h * 16, c * 32 + h * 16 + 16)
                piece = 2.0 * up_acc[rows, n * UW : (n + 1) * UW]
                g_own[c, 2 * h + n, :, AW:PW] = piece
                g_send[c, 2 * h + n, :, AW:PW] = piece.astype(BF)

    for i, d in steps:
        block_copies(i, xf[d], x_dev[d], x)[6].wait_recv()
    for i, step in ((0, 0),) + steps:
        for d in (1, 3, 2):
            bl_copy(i, d, xf[d], lax.rem(xf[d] + 4 - step, 4)).wait_recv()
    for b in range(4):
        back = 2.0 * (bl[0, b] + bl[1, b] + bl[2, b] + bl[3, b])
        blt[:, b * SLOTS : (b + 1) * SLOTS] = back.astype(BF)
    for n in range(2):
        piece = mm(blt[...], hb[:, :, n * AW : (n + 1) * AW].reshape(4 * SLOTS, AW))
        for h in range(2):
            for c in range(2):
                rows = slice(c * 32 + h * 16, c * 32 + h * 16 + 16)
                g_own[c, 2 * h + n, :, 0:AW] = piece[rows]
                g_send[c, 2 * h + n, :, 0:AW] = piece[rows].astype(BF)
    for dc, dy, cc, gg in column:
        send(("ry", dc, dy), g_send.at[cc, ys[dy]], g_recv.at[dc * 4 + dy], at(gg, x, ys[dy], z))

    for d in (1, 3, 2):
        send(("gy", 0, d), sb.at[0, :, ys[d]], yb.at[0, d - 1], y_dev[d])

    def along_y(n):
        for d in (1, 2, 3):
            recv(("gy", n, d), yb.at[n, d - 1], y_dev[d])
        for xx in range(4):
            part = dkv[n, xx, y]
            for d in range(3):
                part += yb[n, d, xx].astype(F32)
            ysum[n, xx] = part
            sb[n, xx, y] = part.astype(BF)
        send(("gz", n), sb.at[n, :, y, half(1 - z)], zr.at[n], z_dev)

    def along_z(n):
        recv(("gz", n), zr.at[n], z_dev)
        for xx in range(4):
            part = ysum[n, xx, half(z), :] + zr[n, xx].astype(F32)
            pf[xx, n] = part.astype(BF)

    along_y(1)
    for dc, dy, cc, gg in column:
        recv(("ry", dc, dy), g_recv.at[dc * 4 + dy], at(gg, x, ys[dy], z))
    part = g_own[core, y]
    for dc, dy, cc, gg in column:
        part += g_recv[dc * 4 + dy].astype(F32)
    here = zl * 2 + z
    z_all[here] = part.astype(BF)
    for dz, e, to, frm, zz in ring:
        send(("rz", dz, e), z_all.at[here], z_all.at[here], at(to * 2 + core, x, y, zz))
    along_y(0)
    along_z(1)
    for dz, e, to, frm, zz in ring:
        recv(("rz", dz, e), z_all.at[frm * 2 + zz], at(to * 2 + core, x, y, zz))
    total = z_all[0].astype(F32)
    for n in range(1, 8):
        total += z_all[n].astype(F32)
    ff[core, x, y] = total.astype(BF)
    for dx, dy in plane:
        send(("fp", dx, dy), ff.at[core, x, y], ff.at[core, x, y], at(g, xs[dx], ys[dy], z))
    along_z(0)
    for d in (1, 3, 2):
        send(("gx", d), pf.at[xs[d]], pr.at[x], x_dev[d])
    pr[x] = pf[x]
    for i, d in steps:
        rd_copy(i, xf[d], x_dev[d]).wait_recv()
    for h in range(4):
        grads_out[128:256, h * D : (h + 1) * D] = rd[h, 0]
        grads_out[256:384, h * D : (h + 1) * D] = rd[h, 1]
    for dx in (0, 1, 3, 2):
        for dy in (0, 1, 3, 2):
            if dx or dy:
                recv(("fp", dx, dy), ff.at[core, xf[dx], yf[dy]], at(g, xs[dx], ys[dy], z))
        send(("fc", dx), ff.at[core, xf[dx]], ff.at[core, xf[dx]], c_dev)
    for d in (1, 2, 3):
        recv(("gx", d), pr.at[xf[d]], x_dev[d])
    for h in range(4):
        grads_out[0:64, h * D : (h + 1) * D] = pr[h, 0]
        grads_out[64:128, h * D : (h + 1) * D] = pr[h, 1]
    ff_out[core] = ff[core]
    for d in range(4):
        recv(("fc", d), ff.at[1 - core, xf[d]], c_dev)
    ff_out[1 - core] = ff[1 - core]

    for c in sent:
        c.wait_send()
    for i, d in steps:
        for c in block_copies(i, x, x_dev[d], xs[d]):
            c.wait_send()
    for i, step in ((0, 0),) + steps:
        for d in (1, 3, 2):
            bl_copy(i, d, x, x).wait_send()
    for i, d in steps:
        rd_copy(i, x, x_dev[0]).wait_send()


def finish(grads, ff, pdk, pdv, rdk, rdv, ga, gu, ff_v, ga_v, gu_v, sem):
    small = [
        pltpu.make_async_copy(grads.at[rows], dst, sem.at[n])
        for n, (rows, dst) in enumerate(
            ((slice(0, 64), pdk), (slice(64, 128), pdv), (slice(128, 256), rdk), (slice(256, 384), rdv))
        )
    ]
    loads = [
        pltpu.make_async_copy(ff.at[:, xx], ff_v.at[:, xx], sem.at[4 + xx]) for xx in range(4)
    ]
    for c in loads + small:
        c.start()
    stores = []
    for xx in range(4):
        loads[xx].wait()
        for c in range(2):
            for p in range(4):
                rows = slice(c * 32 + (p // 2) * 16, c * 32 + (p // 2) * 16 + 16)
                n = 2 * xx + p % 2
                ga_v[rows, n * AW : (n + 1) * AW] = ff_v[c, xx, p, :, 0:AW].astype(F32)
                gu_v[rows, n * UW : (n + 1) * UW] = ff_v[c, xx, p, :, AW:PW].astype(F32)
        for k, (src, dst, w) in enumerate(((ga_v, ga, 2 * AW), (gu_v, gu, 2 * UW))):
            cols = slice(xx * w, (xx + 1) * w)
            c = pltpu.make_async_copy(src.at[:, cols], dst.at[:, cols], sem.at[8 + 2 * xx + k])
            c.start()
            stores.append(c)
    for c in small + stores:
        c.wait()


def body(
    hidden, queries, answer_token_keys, answer_token_values, cotangent, slot_answer_index,
    rewards, group_prompt_keys, group_prompt_values, adapter_down_matrix, adapter_up_matrix,
):
    vmem = pl.BlockSpec(memory_space=pltpu.VMEM)
    hbm = pl.BlockSpec(memory_space=pl.ANY)
    v = pltpu.VMEM
    scratch = [
        v((SLOTS, WIDTH), BF), v((RANK, WIDTH), BF), v((RANK, SPAN), BF), v((SLOTS, FEATURES), BF),
        v((64, D), BF), v((64, D), BF),
        v((2, 64, 512), BF), v((2, 4, 4, 128, D), BF),
        v((4, SLOTS, SPAN), BF), v((4, SLOTS, SPAN), BF), v((4, SLOTS, HW), BF),
        v((4, 2, SLOTS, D), BF), v((4, SLOTS, SLOTS), BF), v((4, RANK, SLOTS), BF), v((SLOTS, FEATURES), BF),
        v((PROMPT + SLOTS, SPAN), F32), v((PROMPT + SLOTS, SPAN), F32),
        v((PROMPT + SLOTS, SPAN), BF), v((D, PROMPT + SLOTS), BF),
        v((2, 4, 4, 128, D), F32), v((4, 4, RANK, SLOTS), F32),
        v((4, 2, SLOTS, D), BF), v((4, 2, SLOTS, D), BF),
        v((RANK, SPAN), F32), v((RANK, 4 * SLOTS), BF),
        v((2, 4, 4, 128, D), BF), v((2, 3, 4, 128, D), BF),
        v((2, 4, 64, D), BF), v((4, 2, 64, D), BF), v((4, 2, 64, D), BF),
        v((2, 4, 128, D), F32),
        v((2, 4, 16, PW), F32), v((2, 4, 16, PW), BF), v((8, 16, PW), BF),
        v((8, 16, PW), BF), v((2, 4, 4, 16, PW), BF),
        pltpu.SemaphoreType.DMA((96,)), pltpu.SemaphoreType.DMA((96,)),
        pltpu.SemaphoreType.DMA((7, 4)), pltpu.SemaphoreType.DMA((7, 4)),
        pltpu.SemaphoreType.DMA((4, 4)), pltpu.SemaphoreType.DMA((4, 4)),
        pltpu.SemaphoreType.DMA((4,)), pltpu.SemaphoreType.DMA((4,)),
        pltpu.SemaphoreType.DMA((10,)),
    ]
    grads, ff = pl.pallas_call(
        kernel,
        out_shape=[
            jax.ShapeDtypeStruct((384, 512), BF),
            jax.ShapeDtypeStruct((2, 4, 4, 16, PW), BF),
        ],
        in_specs=[hbm] * 5 + [vmem] * 2 + [hbm] * 4,
        out_specs=[vmem] * 2,
        scratch_shapes=scratch,
        compiler_params=pltpu.CompilerParams(
            collective_id=0, has_side_effects=True, vmem_limit_bytes=60 << 20
        ),
    )(
        hidden, queries, answer_token_keys, answer_token_values, cotangent,
        slot_answer_index.reshape(1, SLOTS), rewards, group_prompt_keys, group_prompt_values,
        adapter_down_matrix.T, adapter_up_matrix,
    )
    pdk, pdv, rdk, rdv, ga, gu = pl.pallas_call(
        finish,
        out_shape=[
            jax.ShapeDtypeStruct((64, 512), BF), jax.ShapeDtypeStruct((64, 512), BF),
            jax.ShapeDtypeStruct((128, 512), BF), jax.ShapeDtypeStruct((128, 512), BF),
            jax.ShapeDtypeStruct((RANK, WIDTH), F32), jax.ShapeDtypeStruct((RANK, FEATURES), F32),
        ],
        in_specs=[hbm] * 2,
        out_specs=[hbm] * 6,
        scratch_shapes=[
            v((2, 4, 4, 16, PW), BF), v((RANK, WIDTH), F32), v((RANK, FEATURES), F32),
            pltpu.SemaphoreType.DMA((16,)),
        ],
        compiler_params=pltpu.CompilerParams(vmem_limit_bytes=60 << 20),
    )(grads, ff)
    return pdk, pdv, rdk, rdv, ga.T, gu


def solution(mesh):
    rows = P(("grp", "resp"), None)
    in_specs = (
        rows, rows, rows, rows, rows, P(("grp", "resp")), P("grp", None), rows, rows, P(), P(),
    )
    out_specs = (rows, rows, rows, rows, P(), P())
    return jax.shard_map(body, mesh=mesh, in_specs=in_specs, out_specs=out_specs, check_vma=False)
```

time: 126 us -> 123 us (0.976)
  local copies, waits for them, and re-layouts: 10.4 us -> 0 us
  Pallas kernels: 113 us -> 122 us
  other arithmetic: 1.29 us -> 0 us
    pallas_call x1 -> x2, Pallas kernels: 113 us -> 122 us  [the longest x1 109 us: body(): pl.pallas_call(kernel, out_shape=[jax.ShapeDtypeStruct((384, 512), BF), j...]
    convert_element_type x4 -> x0, local copies, waits for them, and re-layouts: 5.46 us -> none  [the longest x2 2.78 us: body(): pieces[..., :AW].transpose(1, 3, 5, 0, 2, 4).reshape(WIDTH, RANK)]
    unnamed x15 -> x0, local copies, waits for them, and re-layouts: 4.91 us -> none
    convert_element_type x2 -> x0, other arithmetic: 1.29 us -> none  [the longest x1 1.16 us: body(): pieces[..., AW:].transpose(0, 2, 4, 1, 3, 5).reshape(RANK, FEATURES)]
where the time goes in v2:
time: 123 us
  Pallas kernels  122 us (99%)
    pallas_call x1, Pallas kernels, body(): pl.pallas_call(kernel, out_shape=[jax.ShapeDtypeStruct((384, 512), BF), j...  109 us
    pallas_call x1, Pallas kernels, body(): pl.pallas_call(finish, out_shape=[jax.ShapeDtypeStruct((64, 512), BF), ja...  13.2 us

profile of v2, /device:TPU:1, one launch (start us, length us, event | category | flops | bytes accessed | tf_op | source)
XLA Modules:
  0.0 122.6 jit_solution(8991756762526463706)
XLA Ops:
  0.6 108.8 %shard_map.154 = (bf16[384,512]{1,0:T(8,128)(2,1)}, bf16[2,4,4,16,1152]{4,3,2,1,0:T(8,128)(2,1)}) custom-call(bf16[128,5120]{1,0:T(8,128)(2,1)} %hidden.1, bf16[128,4096]{1,0:T(8,128)(2,1)} %queries.1, bf16[128,512]{1,0:T(8,128)(2,1)} %ans_k.1, bf16[128,512]{1,0:T(8,128)(2,1)} %ans_v.1, bf16[128,4096]{1,0:T(8,128)(2,1)} %cot.1, s32[1,128]{1,0:T(1,128)} %bitcast.4, ...), custom_call_target="tpu_custom_call" | custom-call | tf_op jit(solution)/shard_map/pallas_call | solution.py:521
  109.4 13.2 %shard_map.155 = (bf16[64,512]{1,0:T(8,128)(2,1)}, bf16[64,512]{1,0:T(8,128)(2,1)}, bf16[128,512]{1,0:T(8,128)(2,1)}, bf16[128,512]{1,0:T(8,128)(2,1)}, f32[64,5120]{1,0:T(8,128)}, /*index=5*/f32[64,4096]{1,0:T(8,128)}) custom-call(bf16[384,512]{1,0:T(8,128)(2,1)} %get-tuple-element.14.grads, bf16[2,4,4,16,1152]{4,3,2,1,0:T(8,128)(2,1)} %get-tuple-element.15.ff), custom_call_target="tpu_custom_call" | custom-call | tf_op jit(solution)/shard_map/pallas_call | solution.py:538

commit v3 on v2

--- a/solution.py
+++ b/solution.py
@@ -43,9 +43,9 @@
     hidden, queries, ans_k, ans_v, cot, slots, rewards, prompt_k, prompt_v, down_t, up,
     grads_out, ff_out,
     hid, down_v, up_v, cot_v, pk, pv, zb, kv, qb, gb, hb, rkv, masks, lows, gfull,
-    s_ref, dp_ref, ds_ref, kt, dkv, bl, rd_send, rd, up_acc, blt,
+    s_ref, dp_ref, ds_ref, kt, dkv, bl, bl_out, rd_send, rd, up_acc, blt,
     sb, yb, zr, pf, pr, ysum,
-    g_own, g_send, g_recv, z_all, ff,
+    a_own, a_send, a_recv, u_own, u_send, u_recv, z_all, ff,
     send_sem, recv_sem, blk_send, blk_recv, bl_send, bl_recv, rd_send_sem, rd_recv_sem, local_sem,
 ):
     g = lax.axis_index("grp")
@@ -72,11 +72,8 @@
             if dz or e:
                 zz = z if e == 0 else 1 - z
                 ring.append((dz, e, lax.rem(zl + dz, 4), lax.rem(zl + 4 - dz, 4), zz))
-    column = []
-    for dc in range(2):
-        for dy in range(4):
-            if dc or dy:
-                column.append((dc, dy, core if dc == 0 else 1 - core, g if dc == 0 else other_g))
+    both = [(dc, dd) for dc in range(2) for dd in (1, 3, 2, 0) if dc or dd]
+    cores, groups = (core, 1 - core), (g, other_g)
     plane = []
     for dx in (0, 1, 3, 2):
         for dy in (0, 1, 3, 2):
@@ -98,12 +95,13 @@
         fetch(6, ans_k.at[:, lanes(x * D, D)], rkv.at[x, 0]),
         fetch(7, ans_v.at[:, lanes(x * D, D)], rkv.at[x, 1]),
         fetch(8, up.at[:, lanes(x * SPAN, SPAN)], up_v),
-        fetch(9, hidden.at[:, lanes(x * HW, HW)], hb.at[x]),
+        fetch(9, hidden.at[:, lanes(y * HW, HW)], hb.at[y]),
     ]
 
     barrier = pltpu.get_barrier_semaphore()
     peers = [at(to * 2 + core, x, y, zz) for dz, e, to, frm, zz in ring]
-    peers += [at(gg, x, ys[dy], z) for dc, dy, cc, gg in column]
+    peers += [at(groups[dc], x, ys[d], z) for dc, d in both]
+    peers += [at(other_g, xs[d], y, z) for d in (1, 2, 3)]
     peers += [at(g, xs[dx], ys[dy], z) for dx, dy in plane if dx]
     for peer in peers:
         pl.semaphore_signal(barrier, inc=1, device_id=peer, device_id_type=mesh_id)
@@ -177,6 +175,30 @@
     loads[2].wait()
     for c in range(0, FEATURES, 512):
         gfull[:, c : c + 512] = (cot_v[:, c : c + 512].astype(F32) * weight).astype(BF)
+
+    def block_copies(i, src, dev, to):
+        pairs = (
+            (queries.at[:, lanes(to * SPAN, SPAN)], qb.at[src]),
+            (gfull.at[:, lanes(to * SPAN, SPAN)], gb.at[src]),
+            (ans_k.at[:, lanes(to * D, D)], rkv.at[src, 0]),
+            (ans_v.at[:, lanes(to * D, D)], rkv.at[src, 1]),
+            (masks.at[x], masks.at[src]),
+            (lows.at[x], lows.at[src]),
+        )
+        return [
+            pltpu.make_async_remote_copy(
+                src_ref=a, dst_ref=b, send_sem=blk_send.at[n, i], recv_sem=blk_recv.at[n, i],
+                device_id=dev, device_id_type=mesh_id,
+            )
+            for n, (a, b) in enumerate(pairs)
+        ]
+
+    def block_send(i, d, which):
+        for c in block_copies(i, x, x_dev[d], xs[d])[which]:
+            c.start()
+
+    block_send(1, 1, slice(0, 5))
+    block_send(2, 3, slice(0, 5))
     x_recv(0, 1, z)
     y_send(0, 1, z)
     recv(("z", 0), zb.at[0], z_dev)
@@ -188,33 +210,9 @@
     x_send(1, 1, zb.at[1], 1 - z)
     kv[1, x, y, half(1 - z), :] = zb[1, :, lanes(x * D, D)]
 
-    def block_copies(i, src, dev, to):
-        pairs = (
-            (queries.at[:, lanes(to * SPAN, SPAN)], qb.at[src]),
-            (gfull.at[:, lanes(to * SPAN, SPAN)], gb.at[src]),
-            (ans_k.at[:, lanes(to * D, D)], rkv.at[src, 0]),
-            (ans_v.at[:, lanes(to * D, D)], rkv.at[src, 1]),
-            (masks.at[x], masks.at[src]),
-            (lows.at[x], lows.at[src]),
-            (hidden.at[:, lanes(to * HW, HW)], hb.at[src]),
-        )
-        return [
-            pltpu.make_async_remote_copy(
-                src_ref=a, dst_ref=b, send_sem=blk_send.at[n, i], recv_sem=blk_recv.at[n, i],
-                device_id=dev, device_id_type=mesh_id,
-            )
-            for n, (a, b) in enumerate(pairs)
-        ]
-
     x_recv(1, 1, 1 - z)
     y_send(1, 1, 1 - z)
     steps = ((1, 1), (2, 3), (3, 2))
-    def block_send(i, d, which):
-        for c in block_copies(i, x, x_dev[d], xs[d])[which]:
-            c.start()
-
-    block_send(1, 1, slice(0, 5))
-    block_send(2, 3, slice(0, 5))
     loads[3].wait()
     loads[4].wait()
     lows[x] = mm(down_v[...], hid[...], NT).astype(BF)
@@ -236,12 +234,15 @@
             device_id=dev, device_id_type=mesh_id,
         )
 
-    def bl_copy(i, d, head, block):
+    def bl_copy(i, d, src):
         return pltpu.make_async_remote_copy(
-            src_ref=bl.at[head, block], dst_ref=bl.at[head, block],
+            src_ref=bl_out.at[i], dst_ref=bl.at[x, y],
             send_sem=bl_send.at[d, i], recv_sem=bl_recv.at[d, i],
-            device_id=x_dev[d], device_id_type=mesh_id,
+            device_id=at(g, src, ys[d], z), device_id_type=mesh_id,
         )
+
+    def hid_copy(d):
+        return copy(("hy", d), hidden.at[:, lanes(ys[d] * HW, HW)], hb.at[y], y_dev[d])
 
     def step_of(i):
         return lax.rem(lax.div(i * (i + 1), 2), 4)
@@ -257,11 +258,8 @@
         @pl.when(i == 1)
         def _():
             block_send(3, 2, slice(0, 5))
-
-        @pl.when(i == 2)
-        def _():
-            for n, d in steps:
-                block_send(n, d, slice(6, 7))
+            for d in (1, 3, 2):
+                hid_copy(d).start()
 
         kt[:, PROMPT:] = rkv[src, 0].T
         mask = masks[src]
@@ -270,22 +268,30 @@
         go = jnp.concatenate([gb[src, :, j * D : (j + 1) * D] for j in range(QH)], axis=0)
 
         def rows(n, c):
-            return rkv[src, n] if c == 16 else kv[n, c // 4, c % 4]
+            if c == 8:
+                return rkv[src, n]
+            return kv[n, c // 2, (c % 2) * 2 : (c % 2) * 2 + 2].reshape(2 * D, D)
 
         def span(c):
-            return slice(c * D, (c + 1) * D)
+            return slice(c * 2 * D, min((c + 1) * 2 * D, PROMPT + SLOTS))
+
+        def gather_rows(n, c, value):
+            if c == 8:
+                rd_send[i, n] = value.astype(BF)
+            else:
+                dkv[n, c // 2, (c % 2) * 2 : (c % 2) * 2 + 2] += value.reshape(2, D, D)
 
         top = None
-        for c in range(17):
+        for c in range(9):
             s = mm(rows(0, c), q, NT)
-            if c == 16:
+            if c == 8:
                 s = jnp.where(mask, s, -1e30)
             s_ref[span(c), :] = s
             part = fold(s, jnp.max)
             top = part if top is None else jnp.maximum(top, part)
         top = jnp.max(top, axis=0, keepdims=True) * LOG2E_FACTOR
         total = None
-        for c in range(17):
+        for c in range(9):
             e = jnp.exp2(s_ref[span(c), :] * LOG2E_FACTOR - top)
             s_ref[span(c), :] = e
             part = fold(e, jnp.sum)
@@ -300,17 +306,13 @@
             y_recv(1, 1, 1 - z)
 
         delta = None
-        for c in range(17):
+        for c in range(9):
             dp = mm(rows(1, c), go, NT)
             pb = (s_ref[span(c), :] * inv).astype(BF)
             dp_ref[span(c), :] = dp
             part = fold(pb.astype(F32) * dp, jnp.sum)
             delta = part if delta is None else delta + part
-            gv = mm(pb, go)
-            if c == 16:
-                rd_send[i, 1] = gv.astype(BF)
-            else:
-                dkv[1, c // 4, c % 4] += gv
+            gather_rows(1, c, mm(pb, go))
         delta = jnp.sum(delta, axis=0, keepdims=True)
         inv = inv * FACTOR
 
@@ -320,27 +322,26 @@
             for d in (1, 3, 2):
                 copy(("gy", 1, d), sb.at[1, :, ys[d]], yb.at[1, d - 1], y_dev[d]).start()
 
-        for c in range(17):
+        for c in range(9):
             ds = (s_ref[span(c), :] * inv * (dp_ref[span(c), :] - delta)).astype(BF)
             ds_ref[span(c), :] = ds
+            gather_rows(0, c, mm(ds, q))
         dq = mm(kt[...], ds_ref[...]).astype(BF)
         back = jnp.zeros((RANK, SLOTS), F32)
         for j in range(QH):
             back += mm(up_v[:, j * D : (j + 1) * D], dq[:, j * D : (j + 1) * D])
-        bl[x, src] = back
+        bl_out[i] = back
         for d in (1, 3, 2):
-            bl_copy(i, d, x, src).start()
+            bl_copy(i, d, src).start()
 
         @pl.when(i > 0)
         def _():
+            bl_copy(i, 0, src).start()
+
+        @pl.when(i > 0)
+        def _():
             block_copies(i, src, at(g, src, y, z), x)[5].wait_recv()
 
-        for c in range(17):
-            gk = mm(ds_ref[span(c), :], q)
-            if c == 16:
-                rd_send[i, 0] = gk.astype(BF)
-            else:
-                dkv[0, c // 4, c % 4] += gk
         low_t = lows[src]
         for j in range(QH):
             up_acc[:, j * D : (j + 1) * D] += mm(low_t, dq[:, j * D : (j + 1) * D], NT)
@@ -355,38 +356,60 @@
     for d in (1, 3, 2):
         sent.append(copy(("gy", 1, d), sb.at[1, :, ys[d]], yb.at[1, d - 1], y_dev[d]))
 
+    for d in (1, 3, 2):
+        sent.append(hid_copy(d))
+    bl[x, y] = bl_out[0]
     rd[x] = rd_send[0]
-    sb[0] = dkv[0].astype(BF)
-    for n in range(2):
+    def pieces(own, out, n, value):
         for h in range(2):
             for c in range(2):
-                rows = slice(c * 32 + h * 16, c * 32 + h * 16 + 16)
-                piece = 2.0 * up_acc[rows, n * UW : (n + 1) * UW]
-                g_own[c, 2 * h + n, :, AW:PW] = piece
-                g_send[c, 2 * h + n, :, AW:PW] = piece.astype(BF)
-
-    for i, d in steps:
-        block_copies(i, xf[d], x_dev[d], x)[6].wait_recv()
+                part = value[c * 32 + h * 16 : c * 32 + h * 16 + 16]
+                own[c, 2 * h + n] = part
+                out[c, 2 * h + n] = part.astype(BF)
+
+    for n in range(2):
+        pieces(u_own, u_send, n, 2.0 * up_acc[:, n * UW : (n + 1) * UW])
+    for dc, d in both:
+        to = at(groups[dc], x, ys[d], z)
+        send(("ru", dc, d), u_send.at[cores[dc], ys[d]], u_recv.at[dc * 4 + d], to)
+    sb[0] = dkv[0].astype(BF)
+
+    for d in (1, 2, 3):
+        recv(("hy", d), hb.at[yf[d]], y_dev[d])
     for i, step in ((0, 0),) + steps:
-        for d in (1, 3, 2):
-            bl_copy(i, d, xf[d], lax.rem(xf[d] + 4 - step, 4)).wait_recv()
+        for d in (1, 3, 2, 0):
+            if i or d:
+                pltpu.make_async_remote_copy(
+                    src_ref=bl_out.at[i], dst_ref=bl.at[xs[step], yf[d]],
+                    send_sem=bl_send.at[d, i], recv_sem=bl_recv.at[d, i],
+                    device_id=at(g, xs[step], yf[d], z), device_id_type=mesh_id,
+                ).wait_recv()
     for b in range(4):
         back = 2.0 * (bl[0, b] + bl[1, b] + bl[2, b] + bl[3, b])
         blt[:, b * SLOTS : (b + 1) * SLOTS] = back.astype(BF)
     for n in range(2):
-        piece = mm(blt[...], hb[:, :, n * AW : (n + 1) * AW].reshape(4 * SLOTS, AW))
-        for h in range(2):
-            for c in range(2):
-                rows = slice(c * 32 + h * 16, c * 32 + h * 16 + 16)
-                g_own[c, 2 * h + n, :, 0:AW] = piece[rows]
-                g_send[c, 2 * h + n, :, 0:AW] = piece[rows].astype(BF)
-    for dc, dy, cc, gg in column:
-        send(("ry", dc, dy), g_send.at[cc, ys[dy]], g_recv.at[dc * 4 + dy], at(gg, x, ys[dy], z))
+        part = mm(blt[...], hb[:, :, n * AW : (n + 1) * AW].reshape(4 * SLOTS, AW))
+        pieces(a_own, a_send, n, part)
+    for dc, d in both:
+        to = at(groups[dc], xs[d], y, z)
+        send(("ra", dc, d), a_send.at[cores[dc], xs[d]], a_recv.at[dc * 4 + d], to)
+    part_u = u_own[core, y]
+    for dc, d in both:
+        recv(("ru", dc, d), u_recv.at[dc * 4 + d], at(groups[dc], x, ys[d], z))
+        part_u += u_recv[dc * 4 + d].astype(F32)
+    part_a = a_own[core, x]
+    for dc, d in both:
+        recv(("ra", dc, d), a_recv.at[dc * 4 + d], at(groups[dc], xs[d], y, z))
+        part_a += a_recv[dc * 4 + d].astype(F32)
+    here = zl * 2 + z
+    z_all[here, :, 0:AW] = part_a.astype(BF)
+    z_all[here, :, AW:PW] = part_u.astype(BF)
+    for dz, e, to, frm, zz in ring:
+        send(("rz", dz, e), z_all.at[here], z_all.at[here], at(to * 2 + core, x, y, zz))
 
     for d in (1, 3, 2):
         send(("gy", 0, d), sb.at[0, :, ys[d]], yb.at[0, d - 1], y_dev[d])
-
-    def along_y(n):
+    for n in (1, 0):
         for d in (1, 2, 3):
             recv(("gy", n, d), yb.at[n, d - 1], y_dev[d])
         for xx in range(4):
@@ -395,26 +418,11 @@
                 part += yb[n, d, xx].astype(F32)
             ysum[n, xx] = part
             sb[n, xx, y] = part.astype(BF)
-        send(("gz", n), sb.at[n, :, y, half(1 - z)], zr.at[n], z_dev)
-
-    def along_z(n):
-        recv(("gz", n), zr.at[n], z_dev)
-        for xx in range(4):
-            part = ysum[n, xx, half(z), :] + zr[n, xx].astype(F32)
-            pf[xx, n] = part.astype(BF)
-
-    along_y(1)
-    for dc, dy, cc, gg in column:
-        recv(("ry", dc, dy), g_recv.at[dc * 4 + dy], at(gg, x, ys[dy], z))
-    part = g_own[core, y]
-    for dc, dy, cc, gg in column:
-        part += g_recv[dc * 4 + dy].astype(F32)
-    here = zl * 2 + z
-    z_all[here] = part.astype(BF)
-    for dz, e, to, frm, zz in ring:
-        send(("rz", dz, e), z_all.at[here], z_all.at[here], at(to * 2 + core, x, y, zz))
-    along_y(0)
-    along_z(1)
+    for i, d in steps:
+        rd_copy(i, xf[d], x_dev[d]).wait_recv()
+    for h in range(4):
+        grads_out[128:256, h * D : (h + 1) * D] = rd[h, 0]
+        grads_out[256:384, h * D : (h + 1) * D] = rd[h, 1]
     for dz, e, to, frm, zz in ring:
         recv(("rz", dz, e), z_all.at[frm * 2 + zz], at(to * 2 + core, x, y, zz))
     total = z_all[0].astype(F32)
@@ -423,15 +431,16 @@
     ff[core, x, y] = total.astype(BF)
     for dx, dy in plane:
         send(("fp", dx, dy), ff.at[core, x, y], ff.at[core, x, y], at(g, xs[dx], ys[dy], z))
-    along_z(0)
+    for n in range(2):
+        send(("gz", n), sb.at[n, :, y, half(1 - z)], zr.at[n], z_dev)
+    for n in range(2):
+        recv(("gz", n), zr.at[n], z_dev)
+        for xx in range(4):
+            part = ysum[n, xx, half(z), :] + zr[n, xx].astype(F32)
+            pf[xx, n] = part.astype(BF)
     for d in (1, 3, 2):
         send(("gx", d), pf.at[xs[d]], pr.at[x], x_dev[d])
     pr[x] = pf[x]
-    for i, d in steps:
-        rd_copy(i, xf[d], x_dev[d]).wait_recv()
-    for h in range(4):
-        grads_out[128:256, h * D : (h + 1) * D] = rd[h, 0]
-        grads_out[256:384, h * D : (h + 1) * D] = rd[h, 1]
     for dx in (0, 1, 3, 2):
         for dy in (0, 1, 3, 2):
             if dx or dy:
@@ -454,38 +463,43 @@
             c.wait_send()
     for i, step in ((0, 0),) + steps:
         for d in (1, 3, 2):
-            bl_copy(i, d, x, x).wait_send()
+            bl_copy(i, d, x).wait_send()
+        if i:
+            bl_copy(i, 0, x).wait_send()
     for i, d in steps:
         rd_copy(i, x, x_dev[0]).wait_send()
 
 
 def finish(grads, ff, pdk, pdv, rdk, rdv, ga, gu, ff_v, ga_v, gu_v, sem):
-    small = [
-        pltpu.make_async_copy(grads.at[rows], dst, sem.at[n])
-        for n, (rows, dst) in enumerate(
-            ((slice(0, 64), pdk), (slice(64, 128), pdv), (slice(128, 256), rdk), (slice(256, 384), rdv))
-        )
+    loads = [
+        pltpu.make_async_copy(ff.at[:, xx], ff_v.at[:, xx], sem.at[xx]) for xx in range(4)
     ]
-    loads = [
-        pltpu.make_async_copy(ff.at[:, xx], ff_v.at[:, xx], sem.at[4 + xx]) for xx in range(4)
-    ]
-    for c in loads + small:
+    for c in loads:
         c.start()
+    pdk[...] = grads[0:64]
+    pdv[...] = grads[64:128]
+    rdk[...] = grads[128:256]
+    rdv[...] = grads[256:384]
     stores = []
     for xx in range(4):
         loads[xx].wait()
         for c in range(2):
+            top = c * 32 + (xx // 2) * 16
             for p in range(4):
                 rows = slice(c * 32 + (p // 2) * 16, c * 32 + (p // 2) * 16 + 16)
-                n = 2 * xx + p % 2
-                ga_v[rows, n * AW : (n + 1) * AW] = ff_v[c, xx, p, :, 0:AW].astype(F32)
+                m, n = 2 * p + xx % 2, 2 * xx + p % 2
+                ga_v[top : top + 16, m * AW : (m + 1) * AW] = ff_v[c, xx, p, :, 0:AW].astype(F32)
                 gu_v[rows, n * UW : (n + 1) * UW] = ff_v[c, xx, p, :, AW:PW].astype(F32)
-        for k, (src, dst, w) in enumerate(((ga_v, ga, 2 * AW), (gu_v, gu, 2 * UW))):
-            cols = slice(xx * w, (xx + 1) * w)
-            c = pltpu.make_async_copy(src.at[:, cols], dst.at[:, cols], sem.at[8 + 2 * xx + k])
-            c.start()
-            stores.append(c)
-    for c in small + stores:
+        cols = slice(2 * xx * UW, 2 * (xx + 1) * UW)
+        done = [(gu_v.at[:, cols], gu.at[:, cols])]
+        if xx % 2:
+            for c in range(2):
+                rows = slice(c * 32 + (xx // 2) * 16, c * 32 + (xx // 2) * 16 + 16)
+                done.append((ga_v.at[rows], ga.at[rows]))
+        for src, dst in done:
+            stores.append(pltpu.make_async_copy(src, dst, sem.at[4 + len(stores)]))
+            stores[-1].start()
+    for c in stores:
         c.wait()
 
 
@@ -504,16 +518,17 @@
         v((4, 2, SLOTS, D), BF), v((4, SLOTS, SLOTS), BF), v((4, RANK, SLOTS), BF), v((SLOTS, FEATURES), BF),
         v((PROMPT + SLOTS, SPAN), F32), v((PROMPT + SLOTS, SPAN), F32),
         v((PROMPT + SLOTS, SPAN), BF), v((D, PROMPT + SLOTS), BF),
-        v((2, 4, 4, 128, D), F32), v((4, 4, RANK, SLOTS), F32),
+        v((2, 4, 4, 128, D), F32), v((4, 4, RANK, SLOTS), F32), v((4, RANK, SLOTS), F32),
         v((4, 2, SLOTS, D), BF), v((4, 2, SLOTS, D), BF),
         v((RANK, SPAN), F32), v((RANK, 4 * SLOTS), BF),
         v((2, 4, 4, 128, D), BF), v((2, 3, 4, 128, D), BF),
         v((2, 4, 64, D), BF), v((4, 2, 64, D), BF), v((4, 2, 64, D), BF),
         v((2, 4, 128, D), F32),
-        v((2, 4, 16, PW), F32), v((2, 4, 16, PW), BF), v((8, 16, PW), BF),
+        v((2, 4, 16, AW), F32), v((2, 4, 16, AW), BF), v((8, 16, AW), BF),
+        v((2, 4, 16, UW), F32), v((2, 4, 16, UW), BF), v((8, 16, UW), BF),
         v((8, 16, PW), BF), v((2, 4, 4, 16, PW), BF),
         pltpu.SemaphoreType.DMA((96,)), pltpu.SemaphoreType.DMA((96,)),
-        pltpu.SemaphoreType.DMA((7, 4)), pltpu.SemaphoreType.DMA((7, 4)),
+        pltpu.SemaphoreType.DMA((6, 4)), pltpu.SemaphoreType.DMA((6, 4)),
         pltpu.SemaphoreType.DMA((4, 4)), pltpu.SemaphoreType.DMA((4, 4)),
         pltpu.SemaphoreType.DMA((4,)), pltpu.SemaphoreType.DMA((4,)),
         pltpu.SemaphoreType.DMA((10,)),
@@ -542,11 +557,11 @@
             jax.ShapeDtypeStruct((128, 512), BF), jax.ShapeDtypeStruct((128, 512), BF),
             jax.ShapeDtypeStruct((RANK, WIDTH), F32), jax.ShapeDtypeStruct((RANK, FEATURES), F32),
         ],
-        in_specs=[hbm] * 2,
-        out_specs=[hbm] * 6,
+        in_specs=[vmem, hbm],
+        out_specs=[vmem] * 4 + [hbm] * 2,
         scratch_shapes=[
             v((2, 4, 4, 16, PW), BF), v((RANK, WIDTH), F32), v((RANK, FEATURES), F32),
-            pltpu.SemaphoreType.DMA((16,)),
+            pltpu.SemaphoreType.DMA((12,)),
         ],
         compiler_params=pltpu.CompilerParams(vmem_limit_bytes=60 << 20),
     )(grads, ff)

time: 123 us -> 110 us (0.89)
  Pallas kernels: 122 us -> 109 us
    pallas_call x1, Pallas kernels: 13.2 us -> 4.22 us  [body(): pl.pallas_call(finish, out_shape=[jax.ShapeDtypeStruct((64, 512), BF), ja...]
    pallas_call x1, Pallas kernels: 109 us -> 105 us  [body(): pl.pallas_call(kernel, out_shape=[jax.ShapeDtypeStruct((384, 512), BF), j...]
where the time goes in v3:
time: 110 us
  Pallas kernels  109 us (99%)
    pallas_call x1, Pallas kernels, body(): pl.pallas_call(kernel, out_shape=[jax.ShapeDtypeStruct((384, 512), BF), j...  105 us
    pallas_call x1, Pallas kernels, body(): pl.pallas_call(finish, out_shape=[jax.ShapeDtypeStruct((64, 512), BF), ja...  4.22 us

profile of v3, /device:TPU:1, one launch (start us, length us, event | category | flops | bytes accessed | tf_op | source)
XLA Modules:
  0.0 109.8 jit_solution(10063278565050774614)
XLA Ops:
  0.6 104.9 %shard_map.154 = (bf16[384,512]{1,0:T(8,128)(2,1)}, bf16[2,4,4,16,1152]{4,3,2,1,0:T(8,128)(2,1)}) custom-call(bf16[128,5120]{1,0:T(8,128)(2,1)} %hidden.1, bf16[128,4096]{1,0:T(8,128)(2,1)} %queries.1, bf16[128,512]{1,0:T(8,128)(2,1)} %ans_k.1, bf16[128,512]{1,0:T(8,128)(2,1)} %ans_v.1, bf16[128,4096]{1,0:T(8,128)(2,1)} %cot.1, s32[1,128]{1,0:T(1,128)} %bitcast.4, ...), custom_call_target="tpu_custom_call" | custom-call | tf_op jit(solution)/shard_map/pallas_call | solution.py:536
  105.6 4.2 %shard_map.155 = (bf16[64,512]{1,0:T(8,128)(2,1)}, bf16[64,512]{1,0:T(8,128)(2,1)}, bf16[128,512]{1,0:T(8,128)(2,1)}, bf16[128,512]{1,0:T(8,128)(2,1)}, f32[64,5120]{1,0:T(8,128)}, /*index=5*/f32[64,4096]{1,0:T(8,128)}) custom-call(bf16[384,512]{1,0:T(8,128)(2,1)} %get-tuple-element.14.grads, bf16[2,4,4,16,1152]{4,3,2,1,0:T(8,128)(2,1)} %get-tuple-element.15.ff), custom_call_target="tpu_custom_call" | custom-call | tf_op jit(solution)/shard_map/pallas_call | solution.py:553

commit v4 on v3

--- a/solution.py
+++ b/solution.py
@@ -197,8 +197,6 @@
         for c in block_copies(i, x, x_dev[d], xs[d])[which]:
             c.start()
 
-    block_send(1, 1, slice(0, 5))
-    block_send(2, 3, slice(0, 5))
     x_recv(0, 1, z)
     y_send(0, 1, z)
     recv(("z", 0), zb.at[0], z_dev)
@@ -206,6 +204,8 @@
     kv[0, x, y, half(1 - z), :] = zb[0, :, lanes(x * D, D)]
     x_recv(1, 0, 1 - z)
     y_send(1, 0, 1 - z)
+    block_send(1, 1, slice(0, 5))
+    block_send(2, 3, slice(0, 5))
     recv(("z", 1), zb.at[1], z_dev)
     x_send(1, 1, zb.at[1], 1 - z)
     kv[1, x, y, half(1 - z), :] = zb[1, :, lanes(x * D, D)]
@@ -451,10 +451,12 @@
     for h in range(4):
         grads_out[0:64, h * D : (h + 1) * D] = pr[h, 0]
         grads_out[64:128, h * D : (h + 1) * D] = pr[h, 1]
-    ff_out[core] = ff[core]
+    stores = [fetch(0, ff.at[core], ff_out.at[core])]
     for d in range(4):
         recv(("fc", d), ff.at[1 - core, xf[d]], c_dev)
-    ff_out[1 - core] = ff[1 - core]
+        stores.append(fetch(1 + d, ff.at[1 - core, xf[d]], ff_out.at[1 - core, xf[d]]))
+    for c in stores:
+        c.wait()
 
     for c in sent:
         c.wait_send()
@@ -540,7 +542,7 @@
             jax.ShapeDtypeStruct((2, 4, 4, 16, PW), BF),
         ],
         in_specs=[hbm] * 5 + [vmem] * 2 + [hbm] * 4,
-        out_specs=[vmem] * 2,
+        out_specs=[vmem, hbm],
         scratch_shapes=scratch,
         compiler_params=pltpu.CompilerParams(
             collective_id=0, has_side_effects=True, vmem_limit_bytes=60 << 20

time: 110 us -> 113 us (1.027)
  Pallas kernels: 109 us -> 112 us
    pallas_call x1, Pallas kernels: 105 us -> 108 us  [body(): pl.pallas_call(kernel, out_shape=[jax.ShapeDtypeStruct((384, 512), BF), j...]
where the time goes in v4:
time: 113 us
  Pallas kernels  112 us (99%)
    pallas_call x1, Pallas kernels, body(): pl.pallas_call(kernel, out_shape=[jax.ShapeDtypeStruct((384, 512), BF), j...  108 us
    pallas_call x1, Pallas kernels, body(): pl.pallas_call(finish, out_shape=[jax.ShapeDtypeStruct((64, 512), BF), ja...  4.22 us

profile of v4, /device:TPU:1, one launch (start us, length us, event | category | flops | bytes accessed | tf_op | source)
XLA Modules:
  0.0 112.8 jit_solution(16020677136255101817)
XLA Ops:
  0.6 108.0 %shard_map.154 = (bf16[384,512]{1,0:T(8,128)(2,1)}, bf16[2,4,4,16,1152]{4,3,2,1,0:T(8,128)(2,1)}) custom-call(bf16[128,5120]{1,0:T(8,128)(2,1)} %hidden.1, bf16[128,4096]{1,0:T(8,128)(2,1)} %queries.1, bf16[128,512]{1,0:T(8,128)(2,1)} %ans_k.1, bf16[128,512]{1,0:T(8,128)(2,1)} %ans_v.1, bf16[128,4096]{1,0:T(8,128)(2,1)} %cot.1, s32[1,128]{1,0:T(1,128)} %bitcast.4, ...), custom_call_target="tpu_custom_call" | custom-call | tf_op jit(solution)/shard_map/pallas_call | solution.py:538
  108.6 4.2 %shard_map.155 = (bf16[64,512]{1,0:T(8,128)(2,1)}, bf16[64,512]{1,0:T(8,128)(2,1)}, bf16[128,512]{1,0:T(8,128)(2,1)}, bf16[128,512]{1,0:T(8,128)(2,1)}, f32[64,5120]{1,0:T(8,128)}, /*index=5*/f32[64,4096]{1,0:T(8,128)}) custom-call(bf16[384,512]{1,0:T(8,128)(2,1)} %get-tuple-element.14.grads, bf16[2,4,4,16,1152]{4,3,2,1,0:T(8,128)(2,1)} %get-tuple-element.15.ff), custom_call_target="tpu_custom_call" | custom-call | tf_op jit(solution)/shard_map/pallas_call | solution.py:555
